TPU v7x, 128 devices: a whole 4x4x4 slice. The times are simulated.
128 devices in a mesh: dp: 16 (over x, y), section: 8 (over z, core).
Axes of the slice: x: 4, y: 4, z: 4, core: 2. Of those that a mesh axis runs over, the one named last changes fastest.
Arguments:
- patches: bfloat16 [16, 256, 1280], P('dp'), may hold values from -6 to 6
- cotangent: bfloat16 [16, 256, 1280], P('dp'), may hold values from -6 to 6
- keep_order: int32 [16, 256], P('dp'), may hold values from 0 to 255, each once within a row
- keep_count: int32 [16], P('dp'), may hold values from 104 to 192, as said below
- destination: int32 [16, 192], P('dp'), may hold values from 0 to 15, as said below
- norm_gain: float32 [16, 1280], P('section'), may hold values from 0.1 to 1.9
- up_blocks: bfloat16 [16, 96, 128, 128], P('section'), may hold values from -0.25 to 0.25
- up_index: int32 [16, 96], P('section'), may hold values from 0 to 199, as said below
- down_blocks: bfloat16 [16, 96, 128, 128], P('section'), may hold values from -0.15625 to 0.15625
- down_index: int32 [16, 96], P('section'), may hold values from 0 to 199, as said below
- layer_count: int32 [8], P('section'), may hold values from 1 to 2, as said below
- regrow_mask: int32 [16, 400], P('section', 'dp'), may hold values 0 or 1
Outputs:
- scores: float32 [16, 400], P('section', 'dp')
Inputs may be any that keep to these rules, and one draw needn't show every extreme that they name: `keep_order`: each row is an ordering of 0 to 255. `keep_count`: some image keeps exactly 192 patches and some exactly 104. `destination`: the kept rows of one replica, image by image and j ascending, are dealt to the replicas in turn from a replica drawn for that replica; so at most 12 of one replica's kept rows go to one replica, and some replica sends exactly 12 to every replica; entries with j >= keep_count are arbitrary. `up_index`: each row lists 96 different block numbers. `down_index`: each row lists 96 different block numbers. `layer_count`: some section uses 2 layers and some uses 1.
All inputs are finite; a program needn't handle non-finite values. No bound on the sum of `regrow_mask` on one device may be relied on, other than what follows from the above.
Results may differ from a plain program's by a relative error of at most 0.0095.
Values may be sent and summed in bfloat16 or wider, within the bound.
A program may use at most 192 MiB of HBM per device.

v0:
```python
import jax
import jax.numpy as jnp
from jax import lax
from jax.sharding import PartitionSpec as P

D = 1280
FF = 2560
BLK = 128
KMAX = 192
LMAX = 2
IMG_DEV = 1
NB = 200


EPS_NORM = 1e-06
EPS_SCORE = 1e-06


def shifted(shard, axis, by):
    count = lax.axis_size(axis)
    pairs = [(i, i + by) for i in range(count) if 0 <= i + by < count]
    return lax.ppermute(shard, axis, pairs)


def dense_matrix(blocks, index, rows, cols):
    edge = blocks.shape[-1]
    total = rows // edge * (cols // edge)
    placed = jnp.zeros((total, edge, edge), blocks.dtype).at[index].set(blocks)
    grid = placed.reshape(rows // edge, cols // edge, edge, edge)
    return grid.transpose(0, 2, 1, 3).reshape(rows, cols)


def to_blocks(matrix, edge):
    rows, cols = matrix.shape
    grid = matrix.reshape(rows // edge, edge, cols // edge, edge)
    return grid.transpose(0, 2, 1, 3).reshape(-1, edge, edge)


def contract_rows(left, right):
    return lax.dot_general(
        left, right, (((0,), (0,)), ((), ())), preferred_element_type=jnp.float32
    )


def contract_cols(left, right):
    return lax.dot_general(
        left, right, (((1,), (1,)), ((), ())), preferred_element_type=jnp.float32
    )


def forward_parts(rows_in, gain, w_up):
    x_float = rows_in.astype(jnp.float32)
    centred = x_float - jnp.mean(x_float, axis=-1, keepdims=True)
    inv_std = lax.rsqrt(jnp.mean(centred * centred, axis=-1, keepdims=True) + EPS_NORM)
    normed = centred * inv_std
    act = (normed * gain).astype(jnp.bfloat16)
    pre = jnp.dot(act, w_up, preferred_element_type=jnp.float32)
    return (x_float, normed, inv_std, act, pre)


def gelu_tanh(values):
    return jax.nn.gelu(values, approximate=True)


def layer_forward(rows_in, gain, w_up, w_down):
    x_float, normed, inv_std, act, pre = forward_parts(rows_in, gain, w_up)
    hidden = gelu_tanh(pre).astype(jnp.bfloat16)
    out = jnp.dot(hidden, w_down, preferred_element_type=jnp.float32)
    return (x_float + out).astype(jnp.bfloat16)


def layer_backward(rows_in, grad_out, gain, w_up, w_down):
    x_float, normed, inv_std, act, pre = forward_parts(rows_in, gain, w_up)
    hidden_float, gelu_back = jax.vjp(gelu_tanh, pre)
    hidden = hidden_float.astype(jnp.bfloat16)
    grad_hidden = contract_cols(grad_out, w_down)
    grad_pre = gelu_back(grad_hidden)[0].astype(jnp.bfloat16)
    grad_normed = contract_cols(grad_pre, w_up) * gain
    grad_norm = inv_std * (
        grad_normed
        - jnp.mean(grad_normed, axis=-1, keepdims=True)
        - normed * jnp.mean(grad_normed * normed, axis=-1, keepdims=True)
    )
    grad_in = (grad_out.astype(jnp.float32) + grad_norm).astype(jnp.bfloat16)
    return (grad_in, act, grad_pre, hidden)


def score_of(summed, rows_total):
    return jnp.sqrt(jnp.mean(summed * summed, axis=(2, 3)) / rows_total + EPS_SCORE)


def body(
    patches,
    cotangent,
    keep_order,
    keep_count,
    destination,
    norm_gain,
    up_blocks,
    up_index,
    down_blocks,
    down_index,
    layer_count,
    regrow_mask,
):
    replicas = lax.axis_size("dp")
    sections = lax.axis_size("section")
    section_id = lax.axis_index("section")
    replica_id = lax.axis_index("dp")
    slots_dev = IMG_DEV * KMAX
    capacity = slots_dev // replicas
    kept = keep_order[:, :KMAX]
    rows_x = jax.vmap(lambda image, order: image[order])(patches, kept).reshape(slots_dev, D)
    rows_ct = jax.vmap(lambda image, order: image[order])(cotangent, kept).reshape(slots_dev, D)
    alive = (jnp.arange(KMAX)[None, :] < keep_count[:, None]).reshape(slots_dev)
    target_id = destination.reshape(slots_dev)
    hits = jnp.logical_and(
        target_id[:, None] == jnp.arange(replicas)[None, :], alive[:, None]
    ).astype(jnp.int32)
    position = jnp.sum((jnp.cumsum(hits, axis=0) - 1) * hits, axis=1)
    landing = jnp.where(alive, target_id * capacity + position, slots_dev)
    send_x = jnp.zeros((slots_dev, D), jnp.bfloat16).at[landing].set(rows_x, mode="drop")
    send_ct = jnp.zeros((slots_dev, D), jnp.bfloat16).at[landing].set(rows_ct, mode="drop")
    inbox_x, inbox_ct = (
        lax.all_to_all(send_x, "dp", split_axis=0, concat_axis=0, tiled=True),
        lax.all_to_all(send_ct, "dp", split_axis=0, concat_axis=0, tiled=True),
    )
    w_up = jax.vmap(lambda blocks, index: dense_matrix(blocks, index, D, FF))(up_blocks, up_index)
    w_down = jax.vmap(lambda blocks, index: dense_matrix(blocks, index, FF, D))(
        down_blocks, down_index
    )
    layer_total = layer_count[0]
    micro = 2
    rows_part = slots_dev // micro
    x_parts = inbox_x.reshape(micro, rows_part, D)
    ct_parts = inbox_ct.reshape(micro, rows_part, D)
    tick_total = micro + sections - 1

    def forward_tick(tick_id, carry):
        incoming, saved = carry
        part_id = tick_id - section_id
        valid = jnp.logical_and(part_id >= 0, part_id < micro)
        safe_id = jnp.clip(part_id, 0, micro - 1)
        first_rows = lax.dynamic_index_in_dim(x_parts, safe_id, 0, keepdims=False)
        current = jnp.where(section_id == 0, first_rows, incoming)

        def advance(state):
            state_rows, store = state
            for slot_id in range(LMAX):
                store = store.at[slot_id, safe_id].set(state_rows)

                def apply_slot(inner_rows, slot_id=slot_id):
                    return layer_forward(
                        inner_rows, norm_gain[slot_id], w_up[slot_id], w_down[slot_id]
                    )

                state_rows = lax.cond(
                    slot_id < layer_total, apply_slot, lambda inner_rows: inner_rows, state_rows
                )
            return (state_rows, store)

        current, saved = lax.cond(valid, advance, lambda state: state, (current, saved))
        incoming = shifted(current, "section", 1)
        return (incoming, saved)

    start_rows = jnp.zeros((rows_part, D), jnp.bfloat16)
    start_saved = jnp.zeros((LMAX, micro, rows_part, D), jnp.bfloat16)
    _, saved = lax.fori_loop(0, tick_total, forward_tick, (start_rows, start_saved))
    live_up = jnp.any(up_index[:, :, None] == jnp.arange(NB)[None, None, :], axis=1)
    live_down = jnp.any(down_index[:, :, None] == jnp.arange(NB)[None, None, :], axis=1)
    live_all = jnp.concatenate([live_up, live_down], axis=1)

    def add_terms(sums, slot_id, act, grad_pre, hidden, grad_out):
        up_sums, down_sums = sums
        return (
            up_sums.at[slot_id].add(contract_rows(act, grad_pre)),
            down_sums.at[slot_id].add(contract_rows(hidden, grad_out)),
        )

    start_sums = (jnp.zeros((LMAX, D, FF), jnp.float32), jnp.zeros((LMAX, FF, D), jnp.float32))

    def backward_tick(tick_id, carry):
        incoming, sums = carry
        part_id = tick_id - (sections - 1 - section_id)
        valid = jnp.logical_and(part_id >= 0, part_id < micro)
        safe_id = jnp.clip(part_id, 0, micro - 1)
        last_rows = lax.dynamic_index_in_dim(ct_parts, safe_id, 0, keepdims=False)
        current = jnp.where(section_id == sections - 1, last_rows, incoming)

        def retreat(state):
            grad_rows, state_sums = state
            for slot_id in reversed(range(LMAX)):

                def apply_back(inner, slot_id=slot_id):
                    grad_value, inner_sums = inner
                    rows_in = lax.dynamic_index_in_dim(saved[slot_id], safe_id, 0, keepdims=False)
                    grad_in, act, grad_pre, hidden = layer_backward(
                        rows_in, grad_value, norm_gain[slot_id], w_up[slot_id], w_down[slot_id]
                    )
                    return (
                        grad_in,
                        add_terms(inner_sums, slot_id, act, grad_pre, hidden, grad_value),
                    )

                grad_rows, state_sums = lax.cond(
                    slot_id < layer_total, apply_back, lambda inner: inner, (grad_rows, state_sums)
                )
            return (grad_rows, state_sums)

        current, sums = lax.cond(valid, retreat, lambda state: state, (current, sums))
        incoming = shifted(current, "section", -1)
        return (incoming, sums)

    _, totals = lax.fori_loop(0, tick_total, backward_tick, (start_rows, start_sums))
    rows_total = float(replicas * slots_dev)
    own_share = 2 * NB // replicas
    own_start = replica_id * own_share
    own_live = lax.dynamic_slice_in_dim(live_all, own_start, own_share, 1)
    up_sums, down_sums = totals
    stacked = jnp.concatenate(
        [
            jax.vmap(lambda matrix: to_blocks(matrix, BLK))(up_sums),
            jax.vmap(lambda matrix: to_blocks(matrix, BLK))(down_sums),
        ],
        axis=1,
    )
    summed = lax.psum_scatter(
        stacked.astype(jnp.bfloat16), "dp", scatter_dimension=1, tiled=True
    ).astype(jnp.float32)
    picked = score_of(summed, rows_total)
    eligible = jnp.logical_and(jnp.logical_not(own_live), regrow_mask == 1)
    return jnp.where(eligible, picked, 0.0)


def solution(mesh):
    return jax.shard_map(
        body,
        mesh=mesh,
        in_specs=(
            P("dp", None, None),
            P("dp", None, None),
            P("dp", None),
            P("dp"),
            P("dp", None),
            P("section", None),
            P("section", None, None, None),
            P("section", None),
            P("section", None, None, None),
            P("section", None),
            P("section"),
            P("section", "dp"),
        ),
        out_specs=P("section", "dp"),
        check_vma=False,
    )
```

profile of v0, /device:TPU:0, one launch (start us, length us, event | category | flops | bytes accessed | tf_op | source)
XLA Modules:
  0.0 1466.3 jit_solution(15993591872043320102)
XLA Ops:
  47.6 31.0 %scatter_fusion.1 = bf16[2,200,128,128]{3,2,1,0:T(8,128)(2,1)} fusion(bf16[2,200,128,128]{3,2,1,0:T(8,128)(2,1)} %broadcast.381.clone.1, s32[192]{0:T(256)S(1)} %reshape.479, bf16[192,128,128]{2,1,0:T(8,128)(2,1)} %bitcast.236), kind=kCustom, calls=%fused_computation.5 | custom fusion | bytes 18875904 | tf_op jit(solution)/shard_map/vmap()/scatter | solution.py:28
  78.6 19.1 %copy.42 = bf16[2,20,128,10,128]{4,3,2,1,0:T(8,128)(2,1)} copy(bf16[2,20,128,10,128]{4,2,3,1,0:T(8,128)(2,1)} %bitcast.227) | data formatting | bytes 26214400 | tf_op jit(solution)/shard_map/while | solution.py:168
  97.7 25.9 %reshape.490 = bf16[2,2560,1280]{2,1,0:T(8,128)(2,1)} reshape(bf16[2,20,128,10,128]{4,3,2,1,0:T(8,128)(2,1)} %copy.42) | data formatting | bytes 26214400 | tf_op jit(solution)/shard_map/while | solution.py:168
  131.8 30.9 %scatter_fusion = bf16[2,200,128,128]{3,2,1,0:T(8,128)(2,1)} fusion(bf16[2,200,128,128]{3,2,1,0:T(8,128)(2,1)} %broadcast.381.clone, s32[192]{0:T(256)S(1)} %reshape.473, bf16[192,128,128]{2,1,0:T(8,128)(2,1)} %bitcast.237), kind=kCustom, calls=%fused_computation.4 | custom fusion | bytes 18875904 | tf_op jit(solution)/shard_map/vmap()/scatter | solution.py:28
  162.7 15.2 %copy.33 = bf16[2,10,128,20,128]{4,3,2,1,0:T(8,128)(2,1)} copy(bf16[2,10,128,20,128]{4,2,3,1,0:T(8,128)(2,1)} %bitcast.226) | data formatting | bytes 26214400 | tf_op jit(solution)/shard_map/vmap()/transpose | solution.py:30
  177.9 22.7 %reshape.433 = bf16[2,1280,2560]{2,1,0:T(8,128)(2,1)} reshape(bf16[2,10,128,20,128]{4,3,2,1,0:T(8,128)(2,1)} %copy.33) | data formatting | bytes 26214400 | tf_op jit(solution)/shard_map/vmap()/reshape | solution.py:30
  200.9 168.2 %while.41 = (s32[]{:T(128)}, bf16[96,1280]{1,0:T(8,128)(2,1)S(1)}, bf16[2,2,96,1280]{3,2,1,0:T(8,128)(2,1)S(1)}, s32[]{:T(128)}, pred[]{:T(512)}, /*index=5*/bf1...) while((s32[]{:T(128)}, bf16[96,1280]{1,0:T(8,128)(2,1)S(1)}, ...), condition=%wide.region_22.23_spmd, body=%wide.region_9.22_spmd.sunk | while | flops 2524815616 | bytes 31908348 | solution.py:168
  201.7 15.4 %conditional.8 = ((bf16[96,1280]{1,0:T(8,128)(2,1)}, bf16[2,2,96,1280]{3,2,1,0:T(8,128)(2,1)S(1)})) conditional(s32[]{:T(128)} %convert_element_type.261, (bf16[96,1280]{1,0:T(8,128)(2,1)}, bf16[2,2,96,1280]{3,2,1,0:T(8,128)(2,1)S(1)}) %tuple.141, (s32[]{:T(128)}, bf16[96,1280]{1,0:T(8,128)(2,1)}, f32[2,1280]{1,0:T(2,128)S(1)}, ...), branch_computations={%region_10.10_spmd, %region_11.21_spmd} | conditional | flops 2524692736 | bytes 30187724 | solution.py:162
  220.4 15.4 %conditional.8 = ((bf16[96,1280]{1,0:T(8,128)(2,1)}, bf16[2,2,96,1280]{3,2,1,0:T(8,128)(2,1)S(1)})) conditional(s32[]{:T(128)} %convert_element_type.261, (bf16[96,1280]{1,0:T(8,128)(2,1)}, bf16[2,2,96,1280]{3,2,1,0:T(8,128)(2,1)S(1)}) %tuple.141, (s32[]{:T(128)}, bf16[96,1280]{1,0:T(8,128)(2,1)}, f32[2,1280]{1,0:T(2,128)S(1)}, ...), branch_computations={%region_10.10_spmd, %region_11.21_spmd} | conditional | flops 2524692736 | bytes 30187724 | solution.py:162
  247.6 27.0 %collective-permute-start = (bf16[96,1280]{1,0:T(8,128)(2,1)}, bf16[96,1280]{1,0:T(8,128)(2,1)S(1)}, u32[]{:S(2)}, u32[]{:S(2)}) collective-permute-start(bf16[96,1280]{1,0:T(8,128)(2,1)} %get-tuple-element.955), channel_id=1, source_target_pairs={{0,1},{1,2},{2,3},{3,4},{4,5},{5,6},{6,7},{8,9},{9,10},{10,11},{11... | collective-permute-start | bytes 737288 | tf_op jit(solution)/shard_map/while/body/eval_jaxpr/ppermute | solution.py:22
  285.1 29.3 %collective-permute-start = (bf16[96,1280]{1,0:T(8,128)(2,1)}, bf16[96,1280]{1,0:T(8,128)(2,1)S(1)}, u32[]{:S(2)}, u32[]{:S(2)}) collective-permute-start(bf16[96,1280]{1,0:T(8,128)(2,1)} %get-tuple-element.955), channel_id=1, source_target_pairs={{0,1},{1,2},{2,3},{3,4},{4,5},{5,6},{6,7},{8,9},{9,10},{10,11},{11... | collective-permute-start | bytes 737288 | tf_op jit(solution)/shard_map/while/body/eval_jaxpr/ppermute | solution.py:22
  324.8 13.2 collective-permute-start
  348.5 19.4 %collective-permute-start = (bf16[96,1280]{1,0:T(8,128)(2,1)}, bf16[96,1280]{1,0:T(8,128)(2,1)S(1)}, u32[]{:S(2)}, u32[]{:S(2)}) collective-permute-start(bf16[96,1280]{1,0:T(8,128)(2,1)} %get-tuple-element.955), channel_id=1, source_target_pairs={{0,1},{1,2},{2,3},{3,4},{4,5},{5,6},{6,7},{8,9},{9,10},{10,11},{11... | collective-permute-start | bytes 737288 | tf_op jit(solution)/shard_map/while/body/eval_jaxpr/ppermute | solution.py:22
  369.2 12.0 broadcast_in_dim.30
  391.5 609.8 %while.42 = (s32[]{:T(128)}, bf16[96,1280]{1,0:T(8,128)(2,1)S(1)}, f32[2,1280,2560]{2,1,0:T(8,128)}, f32[2,2560,1280]{2,1,0:T(8,128)}, s32[]{:T(128)}, /*index=5...) while((s32[]{:T(128)}, bf16[96,1280]{1,0:T(8,128)(2,1)S(1)}, ...), condition=%wide.region_38.39_spmd, body=%wide.region_23.38_spmd.sunk | while | flops 6327050240 | bytes 242327184 | solution.py:214
  400.6 21.2 %collective-permute-done.1 = bf16[96,1280]{1,0:T(8,128)(2,1)S(1)} collective-permute-done((bf16[96,1280]{1,0:T(8,128)(2,1)S(1)}, bf16[96,1280]{1,0:T(8,128)(2,1)S(1)}, u32[]{:S(2)}, u32[]{:S(2)}) %collective-permute-start.1) | collective-permute-done | bytes 245792 | tf_op jit(solution)/shard_map/while/body/eval_jaxpr/ppermute | solution.py:22
  430.7 19.7 %collective-permute-done.1 = bf16[96,1280]{1,0:T(8,128)(2,1)S(1)} collective-permute-done((bf16[96,1280]{1,0:T(8,128)(2,1)S(1)}, bf16[96,1280]{1,0:T(8,128)(2,1)S(1)}, u32[]{:S(2)}, u32[]{:S(2)}) %collective-permute-start.1) | collective-permute-done | bytes 245792 | tf_op jit(solution)/shard_map/while/body/eval_jaxpr/ppermute | solution.py:22
  459.4 21.1 %collective-permute-done.1 = bf16[96,1280]{1,0:T(8,128)(2,1)S(1)} collective-permute-done((bf16[96,1280]{1,0:T(8,128)(2,1)S(1)}, bf16[96,1280]{1,0:T(8,128)(2,1)S(1)}, u32[]{:S(2)}, u32[]{:S(2)}) %collective-permute-start.1) | collective-permute-done | bytes 245792 | tf_op jit(solution)/shard_map/while/body/eval_jaxpr/ppermute | solution.py:22
  481.8 399.5 %collective-permute-done.1 = bf16[96,1280]{1,0:T(8,128)(2,1)S(1)} collective-permute-done((bf16[96,1280]{1,0:T(8,128)(2,1)S(1)}, bf16[96,1280]{1,0:T(8,128)(2,1)S(1)}, u32[]{:S(2)}, u32[]{:S(2)}) %collective-permute-start.1) | collective-permute-done | bytes 245792 | tf_op jit(solution)/shard_map/while/body/eval_jaxpr/ppermute | solution.py:22
  881.4 36.7 %conditional.9 = ((bf16[96,1280]{1,0:T(8,128)(2,1)S(1)}, f32[2,1280,2560]{2,1,0:T(8,128)}, f32[2,2560,1280]{2,1,0:T(8,128)})) conditional(s32[]{:T(128)} %convert_element_type.262, (bf16[96,1280]{1,0:T(8,128)(2,1)S(1)}, f32[2,1280,2560]{2,1,0:T(8,128)}, f32[2,2560,1280]{2,1,0:T(8,128)}) %tuple.144, (s32[]{:T(128)}, ...), branch_computations={%region_24.24_spmd, %region_25.37_spmd} | conditional | flops 6326927360 | bytes 240606512 | solution.py:210
  882.7 35.3 %conditional.4 = ((bf16[96,1280]{1,0:T(8,128)(2,1)S(1)}, f32[2,1280,2560]{2,1,0:T(8,128)}, f32[2,2560,1280]{2,1,0:T(8,128)})) conditional(s32[]{:T(128)} %convert_element_type.109, (bf16[96,1280]{1,0:T(8,128)(2,1)S(1)}, f32[2,1280,2560]{2,1,0:T(8,128)}, f32[2,2560,1280]{2,1,0:T(8,128)}) %get-tuple-element.1080, (bf16[96,1280]{1,0:T(8,128)(2,1)S(1)}, ...), branch_computations={%region_32.31_spmd, %region_33.36_spmd} | conditional | flops 3163463680 | bytes 120303168 | solution.py:205
  919.3 41.6 %collective-permute-done.1 = bf16[96,1280]{1,0:T(8,128)(2,1)S(1)} collective-permute-done((bf16[96,1280]{1,0:T(8,128)(2,1)S(1)}, bf16[96,1280]{1,0:T(8,128)(2,1)S(1)}, u32[]{:S(2)}, u32[]{:S(2)}) %collective-permute-start.1) | collective-permute-done | bytes 245792 | tf_op jit(solution)/shard_map/while/body/eval_jaxpr/ppermute | solution.py:22
  961.0 36.7 %conditional.9 = ((bf16[96,1280]{1,0:T(8,128)(2,1)S(1)}, f32[2,1280,2560]{2,1,0:T(8,128)}, f32[2,2560,1280]{2,1,0:T(8,128)})) conditional(s32[]{:T(128)} %convert_element_type.262, (bf16[96,1280]{1,0:T(8,128)(2,1)S(1)}, f32[2,1280,2560]{2,1,0:T(8,128)}, f32[2,2560,1280]{2,1,0:T(8,128)}) %tuple.144, (s32[]{:T(128)}, ...), branch_computations={%region_24.24_spmd, %region_25.37_spmd} | conditional | flops 6326927360 | bytes 240606512 | solution.py:210
  962.3 35.3 %conditional.4 = ((bf16[96,1280]{1,0:T(8,128)(2,1)S(1)}, f32[2,1280,2560]{2,1,0:T(8,128)}, f32[2,2560,1280]{2,1,0:T(8,128)})) conditional(s32[]{:T(128)} %convert_element_type.109, (bf16[96,1280]{1,0:T(8,128)(2,1)S(1)}, f32[2,1280,2560]{2,1,0:T(8,128)}, f32[2,2560,1280]{2,1,0:T(8,128)}) %get-tuple-element.1080, (bf16[96,1280]{1,0:T(8,128)(2,1)S(1)}, ...), branch_computations={%region_32.31_spmd, %region_33.36_spmd} | conditional | flops 3163463680 | bytes 120303168 | solution.py:205
  1001.3 13.5 convert.19
  1014.8 17.6 %copy.38 = bf16[2,2560,1280]{1,2,0:T(8,128)(2,1)} copy(bf16[2,2560,1280]{2,1,0:T(8,128)(2,1)} %convert.19) | data formatting | bytes 26214400 | tf_op jit(solution)/shard_map/convert.7
  1032.4 22.8 %reshape.438 = bf16[2,20,128,10,128]{2,1,4,3,0:T(8,128)(2,1)} reshape(bf16[2,2560,1280]{1,2,0:T(8,128)(2,1)} %copy.38) | data formatting | bytes 26214400 | tf_op jit(solution)/shard_map/vmap()/reshape | solution.py:35
  1055.1 19.4 %copy.39 = bf16[2,20,10,128,128]{4,3,2,1,0:T(8,128)(2,1)} copy(bf16[2,20,10,128,128]{3,1,4,2,0:T(8,128)(2,1)} %bitcast.228) | data formatting | bytes 26214400 | tf_op jit(solution)/shard_map/vmap()/transpose | solution.py:36
  1074.5 14.9 %convert.18 = bf16[2,1280,2560]{2,1,0:T(8,128)(2,1)} convert(f32[2,1280,2560]{2,1,0:T(8,128)} %get-tuple-element.702) | non-fusion elementwise | flops 6553600 | bytes 39321600 | tf_op jit(solution)/shard_map/convert.10
  1089.4 22.8 %reshape.436 = bf16[2,10,128,20,128]{4,3,2,1,0:T(8,128)(2,1)} reshape(bf16[2,1280,2560]{2,1,0:T(8,128)(2,1)} %convert.18) | data formatting | bytes 26214400 | tf_op jit(solution)/shard_map/vmap()/reshape | solution.py:35
  1123.4 18.3 %pad_maximum_fusion = bf16[2,400,128,128]{3,2,1,0:T(8,128)(2,1)} fusion(bf16[2,200,128,128]{3,2,1,0:T(8,128)(2,1)} %bitcast.230, bf16[2,200,128,128]{3,2,1,0:T(8,128)(2,1)} %bitcast.231), kind=kLoop, calls=%fused_computation.228 | loop fusion | flops 13107200 | bytes 52428800 | tf_op jit(solution)/shard_map/concatenate | solution.py:220
  1143.9 312.5 %all-reduce.4.cloned.1.call-done = bf16[2,400,128,128]{3,2,1,0:T(8,128)(2,1)} async-done(((bf16[2,400,128,128]{3,2,1,0:T(8,128)(2,1)}), bf16[2,400,128,128]{3,2,1,0:T(8,128)(2,1)}) %all-reduce.4.cloned.1.call-update) | async-done | bytes 26214416
  (185 shorter events, 274.5 us)
Async XLA Ops:
  15.2 20.0 %all-to-all-start.1 = ((bf16[16,12,1280]{2,1,0:T(8,128)(2,1)}), bf16[16,12,1280]{2,1,0:T(8,128)(2,1)S(1)}, u32[]{:S(2)}, u32[]{:S(2)}) async-start(bf16[16,12,1280]{2,1,0:T(8,128)(2,1)} %all_to_all.14), calls=%async_computation.1 | async-start | bytes 1310720 | tf_op jit(solution)/shard_map/all_to_all | solution.py:125
  35.2 165.5 %all-to-all-start = ((bf16[16,12,1280]{2,1,0:T(8,128)(2,1)}), bf16[16,12,1280]{2,1,0:T(8,128)(2,1)S(1)}, u32[]{:S(2)}, u32[]{:S(2)}) async-start(bf16[16,12,1280]{2,1,0:T(8,128)(2,1)} %all_to_all.12), calls=%async_computation | async-start | bytes 1310720 | tf_op jit(solution)/shard_map/all_to_all | solution.py:126
  38.8 1417.6 %all-reduce.4.cloned.1.call-start = ((), (), s32[]{:S(2)}) async-start(), calls=%async_computation.2 | async-start | bytes 52428800
  97.7 26.0 %copy-start.3 = (s32[2,96]{1,0:T(2,128)S(1)}, s32[2,96]{1,0:T(2,128)}, u32[]{:S(2)}) copy-start(s32[2,96]{1,0:T(2,128)} %param.47) | copy-start | bytes 2308
  177.9 23.1 %copy-start.2 = (f32[2,1280]{1,0:T(2,128)S(1)}, f32[2,1280]{1,0:T(2,128)}, u32[]{:S(2)}) copy-start(f32[2,1280]{1,0:T(2,128)} %param.45) | copy-start | bytes 30724
  217.0 2.6 collective-permute-start
  235.7 11.2 collective-permute-start
  247.6 28.3 %collective-permute-start = (bf16[96,1280]{1,0:T(8,128)(2,1)}, bf16[96,1280]{1,0:T(8,128)(2,1)S(1)}, u32[]{:S(2)}, u32[]{:S(2)}) collective-permute-start(bf16[96,1280]{1,0:T(8,128)(2,1)} %get-tuple-element.955), channel_id=1, source_target_pairs={{0,1},{1,2},{2,3},{3,4},{4,5},{5,6},{6,7},{8,9},{9,10},{10,11},{11... | collective-permute-start | bytes 737288 | tf_op jit(solution)/shard_map/while/body/eval_jaxpr/ppermute | solution.py:22
  276.6 7.7 collective-permute-start
  285.1 30.7 %collective-permute-start = (bf16[96,1280]{1,0:T(8,128)(2,1)}, bf16[96,1280]{1,0:T(8,128)(2,1)S(1)}, u32[]{:S(2)}, u32[]{:S(2)}) collective-permute-start(bf16[96,1280]{1,0:T(8,128)(2,1)} %get-tuple-element.955), channel_id=1, source_target_pairs={{0,1},{1,2},{2,3},{3,4},{4,5},{5,6},{6,7},{8,9},{9,10},{10,11},{11... | collective-permute-start | bytes 737288 | tf_op jit(solution)/shard_map/while/body/eval_jaxpr/ppermute | solution.py:22
  316.4 7.7 collective-permute-start
  324.8 14.5 collective-permute-start
  340.0 7.7 collective-permute-start
  348.5 20.7 %collective-permute-start = (bf16[96,1280]{1,0:T(8,128)(2,1)}, bf16[96,1280]{1,0:T(8,128)(2,1)S(1)}, u32[]{:S(2)}, u32[]{:S(2)}) collective-permute-start(bf16[96,1280]{1,0:T(8,128)(2,1)} %get-tuple-element.955), channel_id=1, source_target_pairs={{0,1},{1,2},{2,3},{3,4},{4,5},{5,6},{6,7},{8,9},{9,10},{10,11},{11... | collective-permute-start | bytes 737288 | tf_op jit(solution)/shard_map/while/body/eval_jaxpr/ppermute | solution.py:22
  391.8 7.4 collective-permute-start.1
  399.3 22.5 %collective-permute-start.1 = (bf16[96,1280]{1,0:T(8,128)(2,1)S(1)}, bf16[96,1280]{1,0:T(8,128)(2,1)S(1)}, u32[]{:S(2)}, u32[]{:S(2)}) collective-permute-start(bf16[96,1280]{1,0:T(8,128)(2,1)S(1)} %get-tuple-element.969), channel_id=1, source_target_pairs={{1,0},{2,1},{3,2},{4,3},{5,4},{6,5},{7,6},{9,8},{10,9},{11,10},{12... | collective-permute-start | bytes 737288 | tf_op jit(solution)/shard_map/while/body/eval_jaxpr/ppermute | solution.py:22
  421.8 7.5 collective-permute-start.1
  429.4 21.0 %collective-permute-start.1 = (bf16[96,1280]{1,0:T(8,128)(2,1)S(1)}, bf16[96,1280]{1,0:T(8,128)(2,1)S(1)}, u32[]{:S(2)}, u32[]{:S(2)}) collective-permute-start(bf16[96,1280]{1,0:T(8,128)(2,1)S(1)} %get-tuple-element.969), channel_id=1, source_target_pairs={{1,0},{2,1},{3,2},{4,3},{5,4},{6,5},{7,6},{9,8},{10,9},{11,10},{12... | collective-permute-start | bytes 737288 | tf_op jit(solution)/shard_map/while/body/eval_jaxpr/ppermute | solution.py:22
  450.5 7.5 collective-permute-start.1
  458.1 22.4 %collective-permute-start.1 = (bf16[96,1280]{1,0:T(8,128)(2,1)S(1)}, bf16[96,1280]{1,0:T(8,128)(2,1)S(1)}, u32[]{:S(2)}, u32[]{:S(2)}) collective-permute-start(bf16[96,1280]{1,0:T(8,128)(2,1)S(1)} %get-tuple-element.969), channel_id=1, source_target_pairs={{1,0},{2,1},{3,2},{4,3},{5,4},{6,5},{7,6},{9,8},{10,9},{11,10},{12... | collective-permute-start | bytes 737288 | tf_op jit(solution)/shard_map/while/body/eval_jaxpr/ppermute | solution.py:22
  480.5 400.8 %collective-permute-start.1 = (bf16[96,1280]{1,0:T(8,128)(2,1)S(1)}, bf16[96,1280]{1,0:T(8,128)(2,1)S(1)}, u32[]{:S(2)}, u32[]{:S(2)}) collective-permute-start(bf16[96,1280]{1,0:T(8,128)(2,1)S(1)} %get-tuple-element.969), channel_id=1, source_target_pairs={{1,0},{2,1},{3,2},{4,3},{5,4},{6,5},{7,6},{9,8},{10,9},{11,10},{12... | collective-permute-start | bytes 737288 | tf_op jit(solution)/shard_map/while/body/eval_jaxpr/ppermute | solution.py:22
  892.4 23.1 %slice-start.4 = ((s8[13107200]{0:T(1024)(128)(4,1)}), s8[4194304]{0:T(1024)(128)(4,1)S(1)}, s32[]{:S(2)}) async-start(s8[13107200]{0:T(1024)(128)(4,1)} %bitcast.234), calls=%async_computation.7 | async-start | bytes 8388608 | tf_op jit(solution)/shard_map/while/body/eval_jaxpr/cond/branch_1_fun/cond
  892.4 23.1 %slice-start.5 = ((s8[13107200]{0:T(1024)(128)(4,1)}), s8[4194304]{0:T(1024)(128)(4,1)S(1)}, s32[]{:S(2)}) async-start(s8[13107200]{0:T(1024)(128)(4,1)} %bitcast.234), calls=%async_computation.8 | async-start | bytes 8388608 | tf_op jit(solution)/shard_map/while/body/eval_jaxpr/cond/branch_1_fun/cond
  903.9 11.6 slice-start.6
  904.0 11.6 slice-start.7
  918.0 42.9 %collective-permute-start.1 = (bf16[96,1280]{1,0:T(8,128)(2,1)S(1)}, bf16[96,1280]{1,0:T(8,128)(2,1)S(1)}, u32[]{:S(2)}, u32[]{:S(2)}) collective-permute-start(bf16[96,1280]{1,0:T(8,128)(2,1)S(1)} %get-tuple-element.969), channel_id=1, source_target_pairs={{1,0},{2,1},{3,2},{4,3},{5,4},{6,5},{7,6},{9,8},{10,9},{11,10},{12... | collective-permute-start | bytes 737288 | tf_op jit(solution)/shard_map/while/body/eval_jaxpr/ppermute | solution.py:22
  972.0 23.1 %slice-start.4 = ((s8[13107200]{0:T(1024)(128)(4,1)}), s8[4194304]{0:T(1024)(128)(4,1)S(1)}, s32[]{:S(2)}) async-start(s8[13107200]{0:T(1024)(128)(4,1)} %bitcast.234), calls=%async_computation.7 | async-start | bytes 8388608 | tf_op jit(solution)/shard_map/while/body/eval_jaxpr/cond/branch_1_fun/cond
  972.0 23.1 %slice-start.5 = ((s8[13107200]{0:T(1024)(128)(4,1)}), s8[4194304]{0:T(1024)(128)(4,1)S(1)}, s32[]{:S(2)}) async-start(s8[13107200]{0:T(1024)(128)(4,1)} %bitcast.234), calls=%async_computation.8 | async-start | bytes 8388608 | tf_op jit(solution)/shard_map/while/body/eval_jaxpr/cond/branch_1_fun/cond
  983.6 11.6 slice-start.7
  997.7 3.4 collective-permute-start.1
  1141.7 317.2 %copy-start.1 = (bf16[1,256,1280]{2,1,0:T(8,128)(2,1)S(1)}, bf16[1,256,1280]{2,1,0:T(8,128)(2,1)}, u32[]{:S(2)}) copy-start(bf16[1,256,1280]{2,1,0:T(8,128)(2,1)} %param.40) | copy-start | bytes 1966084
  1141.8 316.5 %copy-start.6 = (s32[2,25]{1,0:T(2,128)S(1)}, s32[2,25]{1,0:T(2,128)}, u32[]{:S(2)}) copy-start(s32[2,25]{1,0:T(2,128)} %param.51) | copy-start | bytes 604
  (5 other events, 20.6 us)
Sparse Core Ops, SparseCore 0:
  1142.0 314.4 all-reduce.3
where the time goes:
time: 1480 us; the launch traced here: 1470 us
  waiting for transfers between devices  856 us (58%)
  local copies, waits for them, and re-layouts  289 us (20%)
  starting transfers between devices  142 us (10%)
  matrix products  83.5 us (6%)
  other arithmetic  73.6 us (5%)
  between operations  15.4 us (1%)
    ppermute x18, waiting for transfers between devices, shifted(): return lax.ppermute(shard, axis, pairs)  536 us
    unnamed x2, waiting for transfers between devices  313 us
    ppermute x18, starting transfers between devices, shifted(): return lax.ppermute(shard, axis, pairs)  131 us
    scatter x4, local copies, waits for them, and re-layouts, dense_matrix(): placed = jnp.zeros((total, edge, edge), blocks.dtype).at[index].set(blocks)  62.1 us
    dot_general x4, matrix products, contract_rows(): lax.dot_general(left, right, (((0,), (0,)), ((), ())), preferred_element_...  46.1 us
    reshape x2, local copies, waits for them, and re-layouts, to_blocks(): grid = matrix.reshape(rows // edge, edge, cols // edge, edge)  45.5 us
    while x2, local copies, waits for them, and re-layouts, body(): lax.fori_loop(0, tick_total, forward_tick, (start_rows, start_saved))  45 us
    another operation x5, local copies, waits for them, and re-layouts  33.9 us
  transfers between devices with their start and end apart: 21, of which 20 were waited for; matrix products, arithmetic and copies ran while one was open for 11% of the time, Pallas kernels for 0%

commit v1 on v0

v1 whole, which is shorter than its diff:
```python
import functools
import jax
import jax.numpy as jnp
from jax import lax
from jax.experimental import pallas as pl
from jax.experimental.pallas import tpu as pltpu
from jax.sharding import PartitionSpec as P

D = 1280
FF = 2560
BLK = 128
KMAX = 192
LMAX = 2
NB = 200
NLIVE = 96
NDEAD = NB - NLIVE
UP_COLS = FF // BLK
DOWN_COLS = D // BLK
PARTS = 2 * LMAX
EPS_NORM = 1e-06
EPS_SCORE = 1e-06
MICRO = 2
ROWS = KMAX // MICRO
CHUNK = 512
MESH = pl.DeviceIdType.MESH
F32 = jnp.float32
BF16 = jnp.bfloat16
GELU_A = 0.7978845608028654
GELU_B = 0.044715


def dot(a, b):
    return jnp.dot(a, b, preferred_element_type=F32)


def dot_t(a, b):
    return lax.dot_general(a, b, (((1,), (1,)), ((), ())), preferred_element_type=F32)


def gelu(v):
    return 0.5 * v * (1.0 + jnp.tanh(GELU_A * (v + GELU_B * (v * v * v))))


def gelu_slope(v):
    sq = v * v
    t = jnp.tanh(GELU_A * (v + GELU_B * (v * sq)))
    return 0.5 * (1.0 + t) + 0.5 * v * (1.0 - t * t) * (GELU_A * (1.0 + 3.0 * GELU_B * sq))


def chain_kernel(
    inv_ref, dead_row, dead_col,
    active, pick_ref, patches, cotangent, gain, up_hbm, down_hbm,
    out_hbm,
    stage_a, stage_b, w_up, w_down, xs, gs, normed, inv_std, act, hidden, pre, grad_pre,
    act_t, hidden_t, grad_pre_b, gs_b,
    stage_sem, out_sem, x_send, x_recv, g_send, g_recv,
):
    sections = lax.axis_size("section")
    replica = lax.axis_index("dp")
    section = lax.axis_index("section")
    first = section == 0
    last = section == sections - 1
    stages = (stage_a, stage_b)
    packs = stages

    def flag(l):
        return active[l:l + 1, :1] == 1

    def load(part):
        l, kind = part // 2, part % 2
        src = (up_hbm, down_hbm)[kind].at[l]
        return pltpu.make_async_copy(src, stages[part % 2].at[pl.ds(0, NLIVE)], stage_sem.at[part])

    stage_a[NLIVE] = jnp.zeros((BLK, BLK), BF16)
    stage_b[NLIVE] = jnp.zeros((BLK, BLK), BF16)
    load(0).start()
    load(1).start()

    barrier = pltpu.get_barrier_semaphore()

    @pl.when(jnp.logical_not(first))
    def _():
        pl.semaphore_signal(barrier, inc=1, device_id=(replica, section - 1), device_id_type=MESH)

    @pl.when(jnp.logical_not(last))
    def _():
        pl.semaphore_signal(barrier, inc=1, device_id=(replica, section + 1), device_id_type=MESH)

    @pl.when(jnp.logical_or(first, last))
    def _():
        pl.semaphore_wait(barrier, 1)

    @pl.when(jnp.logical_not(jnp.logical_or(first, last)))
    def _():
        pl.semaphore_wait(barrier, 2)

    def picked(table):
        hot = pick_ref[:, :1] == lax.broadcasted_iota(jnp.int32, (KMAX, table.shape[0]), 1)
        return dot(hot.astype(BF16), table[...]).astype(BF16)

    @pl.when(first)
    def _():
        xs[0] = picked(patches)

    @pl.when(last)
    def _():
        gs[LMAX] = picked(cotangent)

    for part in range(PARTS):
      with jax.named_scope("dense"):
        load(part).wait()
        l, kind = part // 2, part % 2
        target, cols = ((w_up, UP_COLS), (w_down, DOWN_COLS))[kind]

        def place(q, carry, l=l, target=target, cols=cols, part=part):
            rb = q // cols
            cb = q - rb * cols
            target[
                l,
                pl.ds(pl.multiple_of(rb * BLK, BLK), BLK),
                pl.ds(pl.multiple_of(cb * BLK, BLK), BLK),
            ] = stages[part % 2][inv_ref[part * NB + q]]
            return carry

        lax.fori_loop(0, NB, place, 0, unroll=4)
      if part + 2 < PARTS:
        load(part + 2).start()

    def rows_of(mb):
        return pl.ds(pl.multiple_of(mb * ROWS, ROWS), ROWS)

    def cols_of(j, size):
        return pl.ds(pl.multiple_of(j * size, size), size)

    def send_x(mb):
        return pltpu.make_async_remote_copy(
            src_ref=xs.at[LMAX, rows_of(mb)], dst_ref=xs.at[0, rows_of(mb)],
            send_sem=x_send.at[mb], recv_sem=x_recv.at[mb],
            device_id=(replica, section + 1), device_id_type=MESH,
        )

    def send_g(mb):
        return pltpu.make_async_remote_copy(
            src_ref=gs.at[0, rows_of(mb)], dst_ref=gs.at[LMAX, rows_of(mb)],
            send_sem=g_send.at[mb], recv_sem=g_recv.at[mb],
            device_id=(replica, section - 1), device_id_type=MESH,
        )

    def forward(mb, carry):
        r = rows_of(mb)

        @pl.when(jnp.logical_not(first))
        def _():
            send_x(mb).wait_recv()

        for l in range(LMAX):
            x = xs[l, r, :].astype(F32)
            centred = x - jnp.mean(x, axis=-1, keepdims=True)
            inv = lax.rsqrt(jnp.mean(centred * centred, axis=-1, keepdims=True) + EPS_NORM)
            n = centred * inv
            normed[l, r, :] = n
            inv_std[l, r, :] = jnp.broadcast_to(inv, (ROWS, BLK))
            act[l, r, :] = (n * gain[l:l + 1, :]).astype(BF16)

            def up_chunk(j, c, l=l):
                cs = cols_of(j, CHUNK)
                v = dot(act[l, r, :], w_up[l, :, cs])
                pre[l, r, cs] = v
                hidden[l, r, cs] = gelu(v).astype(BF16)
                return c

            with jax.named_scope("f_up"):
                lax.fori_loop(0, FF // CHUNK, up_chunk, 0, unroll=UNROLL)

            def down_chunk(j, c, l=l):
                cs = cols_of(j, 256)
                v = dot(hidden[l, r, :], w_down[l, :, cs])
                had = xs[l, r, cs]
                moved = (had.astype(F32) + v).astype(BF16)
                xs[l + 1, r, cs] = jnp.where(flag(l), moved, had)
                return c

            with jax.named_scope("f_down"):
                lax.fori_loop(0, D // 256, down_chunk, 0, unroll=UNROLL)

        @pl.when(jnp.logical_not(last))
        def _():
            send_x(mb).start()

        return carry

    lax.fori_loop(0, MICRO, forward, 0)

    for l in range(LMAX):
        def slopes(j, c, l=l):
            cs = cols_of(j, BLK)
            pre[l, :, cs] = gelu_slope(pre[l, :, cs])
            h = jnp.where(flag(l), hidden[l, :, cs], jnp.zeros((KMAX, BLK), BF16))
            hidden_t[l, j] = h.T
            return c

        with jax.named_scope("slopes"):
            lax.fori_loop(0, FF // BLK, slopes, 0)

        def turn(j, c, l=l):
            a = jnp.where(flag(l), act[l, :, cols_of(j, BLK)], jnp.zeros((KMAX, BLK), BF16))
            act_t[l, j] = a.T
            return c

        with jax.named_scope("turn"):
            lax.fori_loop(0, D // BLK, turn, 0)

    def backward(mb, carry):
        r = rows_of(mb)

        @pl.when(jnp.logical_not(last))
        def _():
            send_g(mb).wait_recv()

        for l in reversed(range(LMAX)):
            def hidden_chunk(j, c, l=l):
                cs = cols_of(j, CHUNK)
                v = dot_t(gs[l + 1, r, :], w_down[l, cs, :])
                p = (pre[l, r, cs] * v).astype(BF16)
                grad_pre[l, r, cs] = p
                for b in range(CHUNK // BLK):
                    grad_pre_b[l, j * (CHUNK // BLK) + b, r, :] = p[:, b * BLK:(b + 1) * BLK]
                return c

            with jax.named_scope("b_down"):
                lax.fori_loop(0, FF // CHUNK, hidden_chunk, 0, unroll=UNROLL)

            def act_chunk(j, c, l=l):
                cs = cols_of(j, 256)
                v = dot_t(grad_pre[l, r, :], w_up[l, cs, :])
                pre[l, r, cs] = v * gain[l:l + 1, cs]
                return c

            with jax.named_scope("b_up"):
                lax.fori_loop(0, D // 256, act_chunk, 0, unroll=UNROLL)
            u = pre[l, r, :D]
            n = normed[l, r, :]
            step = inv_std[l, r, :1] * (
                u - jnp.mean(u, axis=-1, keepdims=True) - n * jnp.mean(u * n, axis=-1, keepdims=True)
            )
            had = gs[l + 1, r, :]
            for b in range(DOWN_COLS):
                gs_b[l, b, r, :] = had[:, b * BLK:(b + 1) * BLK]
            gs[l, r, :] = jnp.where(flag(l), (had.astype(F32) + step).astype(BF16), had)

        @pl.when(jnp.logical_not(first))
        def _():
            send_g(mb).start()

        return carry

    lax.fori_loop(0, MICRO, backward, 0)

    def store(i):
        l, kind = LMAX - 1 - i // 2, i % 2
        return pltpu.make_async_copy(packs[i % 2], out_hbm.at[l, pl.ds(kind * NDEAD, NDEAD)], out_sem.at[i])

    for i in range(PARTS):
        l, kind = LMAX - 1 - i // 2, i % 2
        if i >= 2:
            store(i - 2).wait()
        left, right = ((act_t, grad_pre_b), (hidden_t, gs_b))[kind]

        def one(k, c, l=l, kind=kind, left=left, right=right, i=i):
            where = (l * 2 + kind) * NDEAD + k
            v = dot(left[l, dead_row[where]], right[l, dead_col[where]])
            packs[i % 2][k] = v.astype(BF16)
            return c

        with jax.named_scope("grads"):
            lax.fori_loop(0, NDEAD, one, 0, unroll=4)
        store(i).start()
    for i in range(PARTS - 2, PARTS):
        store(i).wait()

    def drain(mb, carry):
        @pl.when(jnp.logical_not(last))
        def _():
            send_x(mb).wait_send()

        @pl.when(jnp.logical_not(first))
        def _():
            send_g(mb).wait_send()

        return carry

    lax.fori_loop(0, MICRO, drain, 0)


UNROLL = 1


def chain(inv, dead_row, dead_col, active, pick, patches, cotangent, gain, up, down):
    smem = pl.BlockSpec(memory_space=pltpu.SMEM)
    vmem = pl.BlockSpec(memory_space=pltpu.VMEM)
    hbm = pl.BlockSpec(memory_space=pl.ANY)
    return pl.pallas_call(
        chain_kernel,
        out_shape=jax.ShapeDtypeStruct((LMAX, 2 * NDEAD, BLK, BLK), BF16),
        in_specs=[smem] * 3 + [vmem] * 5 + [hbm] * 2,
        out_specs=hbm,
        scratch_shapes=[
            pltpu.VMEM((NDEAD, BLK, BLK), BF16),
            pltpu.VMEM((NDEAD, BLK, BLK), BF16),
            pltpu.VMEM((LMAX, D, FF), BF16),
            pltpu.VMEM((LMAX, FF, D), BF16),
            pltpu.VMEM((LMAX + 1, KMAX, D), BF16),
            pltpu.VMEM((LMAX + 1, KMAX, D), BF16),
            pltpu.VMEM((LMAX, KMAX, D), F32),
            pltpu.VMEM((LMAX, KMAX, BLK), F32),
            pltpu.VMEM((LMAX, KMAX, D), BF16),
            pltpu.VMEM((LMAX, KMAX, FF), BF16),
            pltpu.VMEM((LMAX, KMAX, FF), F32),
            pltpu.VMEM((LMAX, KMAX, FF), BF16),
            pltpu.VMEM((LMAX, D // BLK, BLK, KMAX), BF16),
            pltpu.VMEM((LMAX, FF // BLK, BLK, KMAX), BF16),
            pltpu.VMEM((LMAX, UP_COLS, KMAX, BLK), BF16),
            pltpu.VMEM((LMAX, DOWN_COLS, KMAX, BLK), BF16),
            pltpu.SemaphoreType.DMA((PARTS,)),
            pltpu.SemaphoreType.DMA((PARTS,)),
            pltpu.SemaphoreType.DMA((MICRO,)),
            pltpu.SemaphoreType.DMA((MICRO,)),
            pltpu.SemaphoreType.DMA((MICRO,)),
            pltpu.SemaphoreType.DMA((MICRO,)),
        ],
        compiler_params=pltpu.CompilerParams(
            collective_id=0, has_side_effects=True, vmem_limit_bytes=60 * 1024 * 1024
        ),
        cost_estimate=pl.CostEstimate(flops=35_000_000_000, bytes_accessed=30_000_000, transcendentals=2_000_000),
    )(inv, dead_row, dead_col, active, pick, patches, cotangent, gain, up, down)


def tables(up_index, down_index):
    listed = jnp.stack([up_index, down_index], axis=1).reshape(PARTS, NLIVE)
    hit = listed[:, :, None] == jnp.arange(NB)[None, None, :]
    live = jnp.any(hit, axis=1)
    inv = jnp.where(live, jnp.sum(jnp.where(hit, jnp.arange(NLIVE)[None, :, None], 0), axis=1), NLIVE)
    q = jnp.arange(NB)
    dead = jnp.logical_not(live)
    rank = jnp.sum((dead[:, :, None] & (q[:, None] < q[None, :])[None]).astype(jnp.int32), axis=1)
    k = jnp.arange(NDEAD)
    at = dead[:, None, :] & (rank[:, None, :] == k[None, :, None])
    number = jnp.sum(jnp.where(at, q[None, None, :], 0), axis=2)
    cols = jnp.array([UP_COLS, DOWN_COLS] * LMAX)[:, None]
    row = number // cols
    return inv.astype(jnp.int32), live, rank, row.astype(jnp.int32), (number - row * cols).astype(jnp.int32)
def body(patches, cotangent, keep_order, keep_count, destination, norm_gain, up_blocks, up_index, down_blocks, down_index, layer_count, regrow_mask):
    replicas = lax.axis_size("dp")
    replica_id = lax.axis_index("dp")
    inv, live, rank, row, col = tables(up_index, down_index)
    kept = jnp.where(jnp.arange(KMAX) < keep_count[0], keep_order[0, :KMAX], -1)
    pick = jnp.broadcast_to(kept[:, None], (KMAX, BLK)).astype(jnp.int32)
    active = jnp.broadcast_to((jnp.arange(8) < layer_count[0])[:, None], (8, BLK)).astype(jnp.int32)
    packed = chain(inv.reshape(-1), row.reshape(-1), col.reshape(-1), active, pick,
                   patches[0], cotangent[0], norm_gain, up_blocks, down_blocks)
    summed = lax.psum_scatter(packed, "dp", scatter_dimension=1, tiled=True).astype(F32)
    rows_total = float(replicas * KMAX)
    own = jnp.sqrt(jnp.mean(summed * summed, axis=(2, 3)) / rows_total + EPS_SCORE)
    every = lax.all_gather(own, "dp", axis=1, tiled=True)
    share = 2 * NB // replicas
    start = replica_id * share
    slot = rank.reshape(LMAX, 2, NB) + (jnp.arange(2) * NDEAD)[None, :, None]
    slot = lax.dynamic_slice_in_dim(slot.reshape(LMAX, 2 * NB), start, share, 1)
    alive = lax.dynamic_slice_in_dim(live.reshape(LMAX, 2 * NB), start, share, 1)
    picked = jnp.sum(jnp.where(slot[:, :, None] == jnp.arange(2 * NDEAD), every[:, None, :], 0.0), axis=2)
    eligible = jnp.logical_and(jnp.logical_not(alive), regrow_mask == 1)
    return jnp.where(eligible, picked, 0.0)


def solution(mesh):
    return jax.shard_map(
        body, mesh=mesh,
        in_specs=(
            P("dp", None, None), P("dp", None, None), P("dp", None), P("dp"), P("dp", None),
            P("section", None), P("section", None, None, None), P("section", None),
            P("section", None, None, None), P("section", None), P("section"), P("section", "dp"),
        ),
        out_specs=P("section", "dp"), check_vma=False,
    )
```

time: 1480 us -> 492 us (0.33)
  waiting for transfers between devices: 856 us -> 186 us
  local copies, waits for them, and re-layouts: 289 us -> 4.25 us
  Pallas kernels: 0 us -> 258 us
  starting transfers between devices: 142 us -> 0.01 us
  matrix products: 83.5 us -> 0 us
  other arithmetic: 73.6 us -> 5.2 us
  blocking collectives: 0 us -> 22.9 us
    ppermute x18 -> x0, waiting for transfers between devices: 536 us -> none  [shifted(): return lax.ppermute(shard, axis, pairs)]
    pallas_call x0 -> x1, Pallas kernels: none -> 258 us  [chain(): pl.pallas_call(chain_kernel, out_shape=jax.ShapeDtypeStruct((LMAX, 2 * ND...]
    ppermute x18 -> x0, starting transfers between devices: 131 us -> none  [shifted(): return lax.ppermute(shard, axis, pairs)]
    unnamed x2, waiting for transfers between devices: 313 us -> 186 us
    dot_general x12 -> x0, matrix products: 83.5 us -> none  [the longest x4 46.1 us: contract_rows(): lax.dot_general(left, right, (((0,), (0,)), ((), ())), preferred_element_...]
    scatter x6 -> x0, local copies, waits for them, and re-layouts: 69.2 us -> none  [the longest x4 62.1 us: dense_matrix(): placed = jnp.zeros((total, edge, edge), blocks.dtype).at[index].set(blocks)]
    reshape x5 -> x2, local copies, waits for them, and re-layouts: 68.5 us -> 0.17 us  [the longest x1 0.09 us: body(): live.reshape(LMAX, 2 * NB)]
    transpose x3 -> x0, local copies, waits for them, and re-layouts: 45.8 us -> none  [the longest x2 30.6 us: to_blocks(): return grid.transpose(0, 2, 1, 3).reshape(-1, edge, edge)]
  transfers between devices with their start and end apart: 21 -> 1, of which waited for: 20 -> 1; matrix products, arithmetic and copies ran while one was open for 11% -> 0% of each run, Pallas kernels for 0% -> 0%
where the time goes in v1:
time: 492 us
  Pallas kernels  258 us (52%)
  waiting for transfers between devices  186 us (38%)
  blocking collectives  22.9 us (5%)
  between operations  15.4 us (3%)
  other arithmetic  5.2 us (1%)
    pallas_call x1, Pallas kernels, chain(): pl.pallas_call(chain_kernel, out_shape=jax.ShapeDtypeStruct((LMAX, 2 * ND...  258 us
    unnamed x2, waiting for transfers between devices  186 us
    all_gather x1, blocking collectives, body(): every = lax.all_gather(own, 'dp', axis=1, tiled=True)  22.9 us
  transfers between devices with their start and end apart: 1, of which 1 were waited for; matrix products, arithmetic and copies ran while one was open for 0% of the time, Pallas kernels for 0%

profile of v1, /device:TPU:0, one launch (start us, length us, event | category | flops | bytes accessed | tf_op | source)
XLA Modules:
  0.0 491.9 jit_solution(9324233452568362536)
XLA Ops:
  6.6 0.7 pad_add_fusion
  7.3 0.1 fusion.1
  7.4 0.1 select_reduce_fusion.1
  7.6 0.2 convert_reduce_fusion
  7.8 0.3 select_reduce_fusion
  8.0 0.1 reduce_sum.50
  8.1 0.7 rem.16
  8.9 0.1 rem.17
  9.0 0.7 select_n.46.inv_ref
  10.9 0.7 multiply_subtract_fusion
  11.6 0.7 compare_select_fusion.1
  12.3 0.7 broadcast_in_dim.82.pick_ref
  13.0 0.7 broadcast_in_dim.80.active
  13.7 258.5 %shard_map.118 = bf16[2,208,128,128]{3,2,1,0:T(8,128)(2,1)} custom-call(s32[800]{0:T(1024)} %select_n.46.inv_ref, s32[416]{0:T(512)} %get-tuple-element.6.dead_row, s32[416]{0:T(512)} %get-tuple-element.5.dead_col, s32[8,128]{1,0:T(8,128)} %broadcast_in_dim.80.active, s32[192,128]{1,0:T(8,128)} %broadcast_in_dim.82.pick_ref, bf16[256,1280]{1,0:T(8,128)(2,1)} %bitcast.31, ...), custom_call_target="tpu_custom_call" | custom-call | flops 35000000512 | bytes 30000000 | tf_op jit(solution)/shard_map/pallas_call | solution.py:302
  272.2 0.0 copy-start.1
  272.2 0.0 all-reduce.3.cloned.1.call-update
  272.2 0.1 reshape.68
  272.3 0.1 reshape.67
  272.4 0.1 add.26
  272.5 0.1 add.27
  272.5 0.1 dynamic-slice.2
  272.6 0.1 dynamic-slice_add_fusion
  272.7 0.1 copy.25
  272.8 0.0 copy-done.1
  272.8 0.6 dynamic-slice
  274.0 185.7 %all-reduce.3.cloned.1.call-done = bf16[2,208,128,128]{3,2,1,0:T(8,128)(2,1)} async-done(((bf16[2,208,128,128]{3,2,1,0:T(8,128)(2,1)}), bf16[2,208,128,128]{3,2,1,0:T(8,128)(2,1)}) %all-reduce.3.cloned.1.call-update) | async-done | bytes 13631504
  459.7 1.4 multiply_reduce_fusion
  461.2 22.9 %all-gather = f32[16,13,2]{1,2,0:T(2,128)S(1)} all-gather(f32[1,13,2]{1,2,0:T(2,128)S(1)} %sqrt_bitcast_fusion), channel_id=1, replica_groups=mesh['dp'=16,'section'=8] {'dp'}, dimensions={0}, use_global_device_ids=true | all-gather | bytes 1768 | tf_op jit(solution)/shard_map/all_gather | solution.py:364
  484.1 0.1 reshape.70
  484.2 0.2 fusion.2
  484.4 0.1 copy.27
  484.5 0.6 and_select_fusion
  (11 shorter events, 0.1 us)
Async XLA Ops:
  6.5 453.2 %all-reduce.3.cloned.1.call-start = ((), (), s32[]{:S(2)}) async-start(), calls=%async_computation | async-start | bytes 27262976
  272.2 0.7 copy-start.1
  272.2 212.3 %copy-start = (s32[2,25]{1,0:T(2,128)S(1)}, s32[2,25]{1,0:T(2,128)}, u32[]{:S(2)}) copy-start(s32[2,25]{1,0:T(2,128)} %param.23) | copy-start | bytes 604
Sparse Core Ops, SparseCore 0:
  272.3 187.3 all-reduce.2

commit v2 on v1

--- a/solution.py
+++ b/solution.py
@@ -17,6 +17,7 @@
 UP_COLS = FF // BLK
 DOWN_COLS = D // BLK
 PARTS = 2 * LMAX
+PANELS = UP_COLS + DOWN_COLS
 EPS_NORM = 1e-06
 EPS_SCORE = 1e-06
 MICRO = 2
@@ -48,12 +49,12 @@
 
 
 def chain_kernel(
-    inv_ref, dead_row, dead_col,
+    inv_ref,
     active, pick_ref, patches, cotangent, gain, up_hbm, down_hbm,
-    out_hbm,
+    left_hbm, right_hbm,
     stage_a, stage_b, w_up, w_down, xs, gs, normed, inv_std, act, hidden, pre, grad_pre,
-    act_t, hidden_t, grad_pre_b, gs_b,
-    stage_sem, out_sem, x_send, x_recv, g_send, g_recv,
+    left, right,
+    stage_sem, left_sem, right_sem, x_send, x_recv, g_send, g_recv,
 ):
     sections = lax.axis_size("section")
     replica = lax.axis_index("dp")
@@ -61,7 +62,6 @@
     first = section == 0
     last = section == sections - 1
     stages = (stage_a, stage_b)
-    packs = stages
 
     def flag(l):
         return active[l:l + 1, :1] == 1
@@ -107,7 +107,6 @@
         gs[LMAX] = picked(cotangent)
 
     for part in range(PARTS):
-      with jax.named_scope("dense"):
         load(part).wait()
         l, kind = part // 2, part % 2
         target, cols = ((w_up, UP_COLS), (w_down, DOWN_COLS))[kind]
@@ -123,8 +122,8 @@
             return carry
 
         lax.fori_loop(0, NB, place, 0, unroll=4)
-      if part + 2 < PARTS:
-        load(part + 2).start()
+        if part + 2 < PARTS:
+            load(part + 2).start()
 
     def rows_of(mb):
         return pl.ds(pl.multiple_of(mb * ROWS, ROWS), ROWS)
@@ -169,8 +168,7 @@
                 hidden[l, r, cs] = gelu(v).astype(BF16)
                 return c
 
-            with jax.named_scope("f_up"):
-                lax.fori_loop(0, FF // CHUNK, up_chunk, 0, unroll=UNROLL)
+            lax.fori_loop(0, FF // CHUNK, up_chunk, 0, unroll=UNROLL)
 
             def down_chunk(j, c, l=l):
                 cs = cols_of(j, 256)
@@ -180,8 +178,7 @@
                 xs[l + 1, r, cs] = jnp.where(flag(l), moved, had)
                 return c
 
-            with jax.named_scope("f_down"):
-                lax.fori_loop(0, D // 256, down_chunk, 0, unroll=UNROLL)
+            lax.fori_loop(0, D // 256, down_chunk, 0, unroll=UNROLL)
 
         @pl.when(jnp.logical_not(last))
         def _():
@@ -190,25 +187,30 @@
         return carry
 
     lax.fori_loop(0, MICRO, forward, 0)
+
+    def save_left(l):
+        return pltpu.make_async_copy(left.at[l], left_hbm.at[l], left_sem.at[l])
 
     for l in range(LMAX):
         def slopes(j, c, l=l):
             cs = cols_of(j, BLK)
             pre[l, :, cs] = gelu_slope(pre[l, :, cs])
             h = jnp.where(flag(l), hidden[l, :, cs], jnp.zeros((KMAX, BLK), BF16))
-            hidden_t[l, j] = h.T
+            left[l, DOWN_COLS + j] = h.T
             return c
 
-        with jax.named_scope("slopes"):
-            lax.fori_loop(0, FF // BLK, slopes, 0)
+        lax.fori_loop(0, FF // BLK, slopes, 0)
 
         def turn(j, c, l=l):
             a = jnp.where(flag(l), act[l, :, cols_of(j, BLK)], jnp.zeros((KMAX, BLK), BF16))
-            act_t[l, j] = a.T
+            left[l, j] = a.T
             return c
 
-        with jax.named_scope("turn"):
-            lax.fori_loop(0, D // BLK, turn, 0)
+        lax.fori_loop(0, D // BLK, turn, 0)
+        save_left(l).start()
+
+    def save_right(l):
+        return pltpu.make_async_copy(right.at[l], right_hbm.at[l], right_sem.at[l])
 
     def backward(mb, carry):
         r = rows_of(mb)
@@ -224,11 +226,10 @@
                 p = (pre[l, r, cs] * v).astype(BF16)
                 grad_pre[l, r, cs] = p
                 for b in range(CHUNK // BLK):
-                    grad_pre_b[l, j * (CHUNK // BLK) + b, r, :] = p[:, b * BLK:(b + 1) * BLK]
+                    right[l, j * (CHUNK // BLK) + b, r, :] = p[:, b * BLK:(b + 1) * BLK]
                 return c
 
-            with jax.named_scope("b_down"):
-                lax.fori_loop(0, FF // CHUNK, hidden_chunk, 0, unroll=UNROLL)
+            lax.fori_loop(0, FF // CHUNK, hidden_chunk, 0, unroll=UNROLL)
 
             def act_chunk(j, c, l=l):
                 cs = cols_of(j, 256)
@@ -236,8 +237,7 @@
                 pre[l, r, cs] = v * gain[l:l + 1, cs]
                 return c
 
-            with jax.named_scope("b_up"):
-                lax.fori_loop(0, D // 256, act_chunk, 0, unroll=UNROLL)
+            lax.fori_loop(0, D // 256, act_chunk, 0, unroll=UNROLL)
             u = pre[l, r, :D]
             n = normed[l, r, :]
             step = inv_std[l, r, :1] * (
@@ -245,7 +245,7 @@
             )
             had = gs[l + 1, r, :]
             for b in range(DOWN_COLS):
-                gs_b[l, b, r, :] = had[:, b * BLK:(b + 1) * BLK]
+                right[l, UP_COLS + b, r, :] = had[:, b * BLK:(b + 1) * BLK]
             gs[l, r, :] = jnp.where(flag(l), (had.astype(F32) + step).astype(BF16), had)
 
         @pl.when(jnp.logical_not(first))
@@ -256,27 +256,8 @@
 
     lax.fori_loop(0, MICRO, backward, 0)
 
-    def store(i):
-        l, kind = LMAX - 1 - i // 2, i % 2
-        return pltpu.make_async_copy(packs[i % 2], out_hbm.at[l, pl.ds(kind * NDEAD, NDEAD)], out_sem.at[i])
-
-    for i in range(PARTS):
-        l, kind = LMAX - 1 - i // 2, i % 2
-        if i >= 2:
-            store(i - 2).wait()
-        left, right = ((act_t, grad_pre_b), (hidden_t, gs_b))[kind]
-
-        def one(k, c, l=l, kind=kind, left=left, right=right, i=i):
-            where = (l * 2 + kind) * NDEAD + k
-            v = dot(left[l, dead_row[where]], right[l, dead_col[where]])
-            packs[i % 2][k] = v.astype(BF16)
-            return c
-
-        with jax.named_scope("grads"):
-            lax.fori_loop(0, NDEAD, one, 0, unroll=4)
-        store(i).start()
-    for i in range(PARTS - 2, PARTS):
-        store(i).wait()
+    for l in range(LMAX):
+        save_right(l).start()
 
     def drain(mb, carry):
         @pl.when(jnp.logical_not(last))
@@ -290,23 +271,29 @@
         return carry
 
     lax.fori_loop(0, MICRO, drain, 0)
-
-
-UNROLL = 1
-
-
-def chain(inv, dead_row, dead_col, active, pick, patches, cotangent, gain, up, down):
+    for l in range(LMAX):
+        save_left(l).wait()
+        save_right(l).wait()
+
+
+UNROLL = True
+
+
+def chain(inv, active, pick, patches, cotangent, gain, up, down):
     smem = pl.BlockSpec(memory_space=pltpu.SMEM)
     vmem = pl.BlockSpec(memory_space=pltpu.VMEM)
     hbm = pl.BlockSpec(memory_space=pl.ANY)
     return pl.pallas_call(
         chain_kernel,
-        out_shape=jax.ShapeDtypeStruct((LMAX, 2 * NDEAD, BLK, BLK), BF16),
-        in_specs=[smem] * 3 + [vmem] * 5 + [hbm] * 2,
-        out_specs=hbm,
+        out_shape=(
+            jax.ShapeDtypeStruct((LMAX, PANELS, BLK, KMAX), BF16),
+            jax.ShapeDtypeStruct((LMAX, PANELS, KMAX, BLK), BF16),
+        ),
+        in_specs=[smem] + [vmem] * 5 + [hbm] * 2,
+        out_specs=(hbm, hbm),
         scratch_shapes=[
-            pltpu.VMEM((NDEAD, BLK, BLK), BF16),
-            pltpu.VMEM((NDEAD, BLK, BLK), BF16),
+            pltpu.VMEM((NLIVE + 1, BLK, BLK), BF16),
+            pltpu.VMEM((NLIVE + 1, BLK, BLK), BF16),
             pltpu.VMEM((LMAX, D, FF), BF16),
             pltpu.VMEM((LMAX, FF, D), BF16),
             pltpu.VMEM((LMAX + 1, KMAX, D), BF16),
@@ -317,12 +304,11 @@
             pltpu.VMEM((LMAX, KMAX, FF), BF16),
             pltpu.VMEM((LMAX, KMAX, FF), F32),
             pltpu.VMEM((LMAX, KMAX, FF), BF16),
-            pltpu.VMEM((LMAX, D // BLK, BLK, KMAX), BF16),
-            pltpu.VMEM((LMAX, FF // BLK, BLK, KMAX), BF16),
-            pltpu.VMEM((LMAX, UP_COLS, KMAX, BLK), BF16),
-            pltpu.VMEM((LMAX, DOWN_COLS, KMAX, BLK), BF16),
+            pltpu.VMEM((LMAX, PANELS, BLK, KMAX), BF16),
+            pltpu.VMEM((LMAX, PANELS, KMAX, BLK), BF16),
             pltpu.SemaphoreType.DMA((PARTS,)),
-            pltpu.SemaphoreType.DMA((PARTS,)),
+            pltpu.SemaphoreType.DMA((LMAX,)),
+            pltpu.SemaphoreType.DMA((LMAX,)),
             pltpu.SemaphoreType.DMA((MICRO,)),
             pltpu.SemaphoreType.DMA((MICRO,)),
             pltpu.SemaphoreType.DMA((MICRO,)),
@@ -332,7 +318,7 @@
             collective_id=0, has_side_effects=True, vmem_limit_bytes=60 * 1024 * 1024
         ),
         cost_estimate=pl.CostEstimate(flops=35_000_000_000, bytes_accessed=30_000_000, transcendentals=2_000_000),
-    )(inv, dead_row, dead_col, active, pick, patches, cotangent, gain, up, down)
+    )(inv, active, pick, patches, cotangent, gain, up, down)
 
 
 def tables(up_index, down_index):
@@ -348,20 +334,245 @@
     number = jnp.sum(jnp.where(at, q[None, None, :], 0), axis=2)
     cols = jnp.array([UP_COLS, DOWN_COLS] * LMAX)[:, None]
     row = number // cols
-    return inv.astype(jnp.int32), live, rank, row.astype(jnp.int32), (number - row * cols).astype(jnp.int32)
-def body(patches, cotangent, keep_order, keep_count, destination, norm_gain, up_blocks, up_index, down_blocks, down_index, layer_count, regrow_mask):
+    col = number - row * cols
+    base = jnp.arange(PARTS)[:, None] % 2
+    row = (row + base * DOWN_COLS).astype(jnp.int32)
+    col = (col + base * UP_COLS).astype(jnp.int32)
+    return inv.astype(jnp.int32), live, rank, row, col
+
+
+RING = 4
+PER = 2 * NDEAD // (RING * RING)
+HALF = BLK // 2
+TILE = 32
+
+
+def sums_kernel(
+    dead_row, dead_col, left_hbm, right_hbm, out_ref,
+    left_0, left_1, right_0, right_1,
+    opp_0, opp_1, nxt_0, nxt_1, prv_0, prv_1, mid_0, mid_1,
+    ra_0, ra_1, rb_0, rb_1, ia_0, ia_1, ib_0, ib_1,
+    sa_0, sa_1, sb_0, sb_1, ja_0, ja_1, jb_0, jb_1,
+    squares, mine, row_tiles, all_tiles,
+    load_sem, send_sem, recv_sem, tile_send, tile_recv, full_send, full_recv,
+):
+    section = lax.axis_index("section")
+    replica = lax.axis_index("dp")
+    px = replica // RING
+    py = lax.rem(replica, RING)
+
+    def peer(axis, step):
+        if axis == 0:
+            return (lax.rem(px + step, RING) * RING + py, section)
+        return (px * RING + lax.rem(py + step, RING), section)
+
+    lefts, rights = (left_1, left_0), (right_1, right_0)
+
+    def load(h):
+        l = LMAX - 1 - h
+        return (
+            pltpu.make_async_copy(left_hbm.at[l], lefts[h], load_sem.at[h, 0]),
+            pltpu.make_async_copy(right_hbm.at[l], rights[h], load_sem.at[h, 1]),
+        )
+
+    for h in range(2):
+        for copy in load(h):
+            copy.start()
+
+    barrier = pltpu.get_barrier_semaphore()
+    for axis in range(2):
+        for step in range(1, RING):
+            pl.semaphore_signal(barrier, inc=1, device_id=peer(axis, step), device_id_type=MESH)
+    pl.semaphore_wait(barrier, 2 * (RING - 1))
+    for h in range(2):
+        for copy in load(h):
+            copy.wait()
+
+    opp, nxt, prv, mid = (opp_0, opp_1), (nxt_0, nxt_1), (prv_0, prv_1), (mid_0, mid_1)
+    ra, rb, ia, ib = (ra_0, ra_1), (rb_0, rb_1), (ia_0, ia_1), (ib_0, ib_1)
+    sa, sb, ja, jb = (sa_0, sa_1), (sb_0, sb_1), (ja_0, ja_1), (jb_0, jb_1)
+    place = (px, py)
+
+    def at(axis, step):
+        return lax.rem(place[axis] + step, RING)
+
+    def block(h, f, c, g):
+        where = (LMAX - 1 - h) * 2 * NDEAD + (f * PER + c) * RING + g
+        return dot(lefts[h][dead_row[where]], rights[h][dead_col[where]])
+
+    def send(h, kind, c, src, dst, axis, step):
+        return pltpu.make_async_remote_copy(
+            src_ref=src, dst_ref=dst, send_sem=send_sem.at[h, kind, c], recv_sem=recv_sem.at[h, kind, c],
+            device_id=peer(axis, step), device_id_type=MESH,
+        )
+
+    def copies(h, c):
+        first, second = h, 1 - h
+        far = at(second, 2)
+        return (
+            send(h, 0, c, opp[h].at[c, pl.ds(0, 2)], ra[h].at[c], first, 1),
+            send(h, 1, c, opp[h].at[c, pl.ds(2, 2)], rb[h].at[c], first, 3),
+            send(h, 2, c, nxt[h].at[c], ia[h].at[c], first, 1),
+            send(h, 3, c, prv[h].at[c], ib[h].at[c], first, 3),
+            send(h, 4, c, mid[h].at[c, far, pl.ds(0, HALF)], sa[h].at[c], second, 1),
+            send(h, 5, c, mid[h].at[c, far, pl.ds(HALF, HALF)], sb[h].at[c], second, 3),
+            send(h, 6, c, mid[h].at[c, at(second, 1)], ja[h].at[c], second, 1),
+            send(h, 7, c, mid[h].at[c, at(second, 3)], jb[h].at[c], second, 3),
+        )
+
+    def far_units(c, carry):
+        for h in range(2):
+            for g in range(RING):
+                opp[h][c, g] = block(h, at(h, 2), c, g).astype(BF16)
+            moves = copies(h, c)
+            moves[0].start()
+            moves[1].start()
+        return carry
+
+    def near_units(c, carry):
+        for h in range(2):
+            moves = copies(h, c)
+            ahead = [block(h, at(h, 1), c, g) for g in range(RING)]
+            behind = [block(h, at(h, 3), c, g) for g in range(RING)]
+            moves[0].wait_recv()
+            for g in range(RING):
+                v = ahead[g] + ra[h][c, g].astype(F32) if g < 2 else ahead[g]
+                nxt[h][c, g] = v.astype(BF16)
+            moves[2].start()
+            moves[1].wait_recv()
+            for g in range(RING):
+                v = behind[g] + rb[h][c, g - 2].astype(F32) if g >= 2 else behind[g]
+                prv[h][c, g] = v.astype(BF16)
+            moves[3].start()
+        return carry
+
+    def own_units(c, carry):
+        for h in range(2):
+            moves = copies(h, c)
+            own = [block(h, place[h], c, g) for g in range(RING)]
+            moves[2].wait_recv()
+            moves[3].wait_recv()
+            for g in range(RING):
+                v = own[g] + ia[h][c, g].astype(F32) + ib[h][c, g].astype(F32)
+                mid[h][c, g] = v.astype(BF16)
+            moves[4].start()
+            moves[5].start()
+        return carry
+
+    def second_axis(c, carry):
+        for h in range(2):
+            moves = copies(h, c)
+            ahead, behind = at(1 - h, 1), at(1 - h, 3)
+            moves[4].wait_recv()
+            top = pl.ds(0, HALF)
+            v = mid[h][c, ahead, top, :].astype(F32) + sa[h][c].astype(F32)
+            mid[h][c, ahead, top, :] = v.astype(BF16)
+            moves[6].start()
+            moves[5].wait_recv()
+            low = pl.ds(HALF, HALF)
+            v = mid[h][c, behind, low, :].astype(F32) + sb[h][c].astype(F32)
+            mid[h][c, behind, low, :] = v.astype(BF16)
+            moves[7].start()
+        return carry
+
+    def totals(c, carry):
+        for h in range(2):
+            moves = copies(h, c)
+            moves[6].wait_recv()
+            moves[7].wait_recv()
+            v = mid[h][c, place[1 - h]].astype(F32) + ja[h][c].astype(F32) + jb[h][c].astype(F32)
+            squares[h, pl.ds(c, 1), :] = jnp.sum(v * v, axis=0, keepdims=True)
+        return carry
+
+    def drain(c, carry):
+        for h in range(2):
+            for move in copies(h, c):
+                move.wait_send()
+        return carry
+
+    squares[...] = jnp.zeros_like(squares)
+    for step in (far_units, near_units, own_units, second_axis, totals):
+        lax.fori_loop(0, PER, step, 0)
+    rows_total = float(RING * RING * KMAX)
+    mean = jnp.sum(squares[...].reshape(TILE, BLK), axis=1, keepdims=True) * (1.0 / (BLK * BLK))
+    mine[...] = jnp.broadcast_to(jnp.sqrt(mean / rows_total + EPS_SCORE), (TILE, BLK))
+
+    row_tiles[px] = mine[...]
+    rows = [
+        pltpu.make_async_remote_copy(
+            src_ref=mine, dst_ref=row_tiles.at[px], send_sem=tile_send.at[step - 1],
+            recv_sem=tile_recv.at[step - 1], device_id=peer(0, step), device_id_type=MESH,
+        )
+        for step in range(1, RING)
+    ]
+    for move in rows:
+        move.start()
+    for move in rows:
+        move.wait()
+    all_tiles[py] = row_tiles[...]
+    cols = [
+        pltpu.make_async_remote_copy(
+            src_ref=row_tiles, dst_ref=all_tiles.at[py], send_sem=full_send.at[step - 1],
+            recv_sem=full_recv.at[step - 1], device_id=peer(1, step), device_id_type=MESH,
+        )
+        for step in range(1, RING)
+    ]
+    for move in cols:
+        move.start()
+    for move in cols:
+        move.wait()
+    out_ref[...] = all_tiles[...]
+    lax.fori_loop(0, PER, drain, 0)
+
+
+def sums(dead_row, dead_col, left, right):
+    smem = pl.BlockSpec(memory_space=pltpu.SMEM)
+    hbm = pl.BlockSpec(memory_space=pl.ANY)
+
+    def blocks(*lead):
+        return [pltpu.VMEM((PER, *lead, BLK), BF16)] * 2
+
+    return pl.pallas_call(
+        sums_kernel,
+        out_shape=jax.ShapeDtypeStruct((RING, RING, TILE, BLK), F32),
+        in_specs=[smem] * 2 + [hbm] * 2,
+        out_specs=pl.BlockSpec(memory_space=pltpu.VMEM),
+        scratch_shapes=[
+            *[pltpu.VMEM((PANELS, BLK, KMAX), BF16)] * 2,
+            *[pltpu.VMEM((PANELS, KMAX, BLK), BF16)] * 2,
+            *blocks(RING, BLK), *blocks(RING, BLK), *blocks(RING, BLK), *blocks(RING, BLK),
+            *blocks(2, BLK), *blocks(2, BLK), *blocks(RING, BLK), *blocks(RING, BLK),
+            *blocks(HALF), *blocks(HALF), *blocks(BLK), *blocks(BLK),
+            pltpu.VMEM((2, TILE // 2, BLK), F32),
+            pltpu.VMEM((TILE, BLK), F32),
+            pltpu.VMEM((RING, TILE, BLK), F32),
+            pltpu.VMEM((RING, RING, TILE, BLK), F32),
+            pltpu.SemaphoreType.DMA((2, 2)),
+            pltpu.SemaphoreType.DMA((2, 8, PER)),
+            pltpu.SemaphoreType.DMA((2, 8, PER)),
+            *[pltpu.SemaphoreType.DMA((RING - 1,))] * 4,
+        ],
+        compiler_params=pltpu.CompilerParams(
+            collective_id=1, has_side_effects=True, vmem_limit_bytes=60 * 1024 * 1024
+        ),
+        cost_estimate=pl.CostEstimate(flops=3_000_000_000, bytes_accessed=8_000_000, transcendentals=0),
+    )(dead_row, dead_col, left, right)
+
+
+def body(patches, cotangent, keep_order, keep_count, destination, norm_gain, up_blocks, up_index,
+         down_blocks, down_index, layer_count, regrow_mask):
     replicas = lax.axis_size("dp")
     replica_id = lax.axis_index("dp")
     inv, live, rank, row, col = tables(up_index, down_index)
     kept = jnp.where(jnp.arange(KMAX) < keep_count[0], keep_order[0, :KMAX], -1)
     pick = jnp.broadcast_to(kept[:, None], (KMAX, BLK)).astype(jnp.int32)
     active = jnp.broadcast_to((jnp.arange(8) < layer_count[0])[:, None], (8, BLK)).astype(jnp.int32)
-    packed = chain(inv.reshape(-1), row.reshape(-1), col.reshape(-1), active, pick,
-                   patches[0], cotangent[0], norm_gain, up_blocks, down_blocks)
-    summed = lax.psum_scatter(packed, "dp", scatter_dimension=1, tiled=True).astype(F32)
-    rows_total = float(replicas * KMAX)
-    own = jnp.sqrt(jnp.mean(summed * summed, axis=(2, 3)) / rows_total + EPS_SCORE)
-    every = lax.all_gather(own, "dp", axis=1, tiled=True)
+    left, right = chain(inv.reshape(-1), active, pick, patches[0], cotangent[0], norm_gain, up_blocks, down_blocks)
+    tiles = sums(row.reshape(-1), col.reshape(-1), left, right)
+    half = TILE // 2
+    late = tiles[:, :, :PER, 0].transpose(1, 2, 0).reshape(2 * NDEAD)
+    early = tiles[:, :, half:half + PER, 0].transpose(0, 2, 1).reshape(2 * NDEAD)
+    every = jnp.stack([early, late])
     share = 2 * NB // replicas
     start = replica_id * share
     slot = rank.reshape(LMAX, 2, NB) + (jnp.arange(2) * NDEAD)[None, :, None]

time: 492 us -> 277 us (0.56)
  waiting for transfers between devices: 186 us -> 0 us
  blocking collectives: 22.9 us -> 0 us
  between operations: 15.4 us -> 1.42 us
  Pallas kernels: 258 us -> 266 us
    unnamed x2 -> x0, waiting for transfers between devices: 186 us -> none
    all_gather x1 -> x0, blocking collectives: 22.9 us -> none  [body(): every = lax.all_gather(own, 'dp', axis=1, tiled=True)]
    pallas_call x1 -> x2, Pallas kernels: 258 us -> 266 us  [the longest x1 182 us: chain(): pl.pallas_call(chain_kernel, out_shape=(jax.ShapeDtypeStruct((LMAX, PANEL...]
  transfers between devices with their start and end apart: 1 -> 0, of which waited for: 1 -> 0; matrix products, arithmetic and copies ran while one was open for 0% -> 0% of each run, Pallas kernels for 0% -> 0%
where the time goes in v2:
time: 277 us
  Pallas kernels  266 us (96%)
  local copies, waits for them, and re-layouts  5.44 us (2%)
  other arithmetic  3.81 us (1%)
    pallas_call x1, Pallas kernels, chain(): pl.pallas_call(chain_kernel, out_shape=(jax.ShapeDtypeStruct((LMAX, PANEL...  182 us
    pallas_call x1, Pallas kernels, sums(): pl.pallas_call(sums_kernel, out_shape=jax.ShapeDtypeStruct((RING, RING, T...  83.6 us

profile of v2, /device:TPU:0, one launch (start us, length us, event | category | flops | bytes accessed | tf_op | source)
XLA Modules:
  0.0 276.7 jit_solution(15333163405342718016)
XLA Ops:
  0.0 0.7 pad_add_fusion
  0.7 0.1 fusion.1
  0.9 0.2 convert_reduce_fusion
  1.1 0.3 select_reduce_fusion
  1.4 0.1 reduce_sum.40
  1.5 0.1 add.64
  1.5 0.1 add.65
  1.7 0.1 add.68
  1.8 0.7 rem.31
  2.5 0.1 rem.32
  2.6 0.7 subtract_add_fusion
  3.3 0.1 select_reduce_fusion.1
  3.5 0.7 select_n.66.inv_ref
  4.8 0.7 compare_select_fusion.1
  5.5 0.7 broadcast_in_dim.83.pick_ref
  6.9 0.7 broadcast_in_dim.81.active
  7.5 182.4 %shard_map.118 = (bf16[2,30,128,192]{3,2,1,0:T(8,128)(2,1)}, bf16[2,30,192,128]{3,2,1,0:T(8,128)(2,1)}) custom-call(s32[800]{0:T(1024)} %select_n.66.inv_ref, s32[8,128]{1,0:T(8,128)} %broadcast_in_dim.81.active, s32[192,128]{1,0:T(8,128)} %broadcast_in_dim.83.pick_ref, bf16[256,1280]{1,0:T(8,128)(2,1)} %bitcast.20, bf16[256,1280]{1,0:T(8,128)(2,1)} %bitcast.21, ...), custom_call_target="tpu_custom_call" | custom-call | flops 35000000512 | bytes 30000000 | tf_op jit(solution)/shard_map/pallas_call | solution.py:286
  189.9 83.6 %shard_map.119 = f32[4,4,32,128]{3,2,1,0:T(8,128)} custom-call(s32[416]{0:T(512)} %get-tuple-element.12.dead_row, s32[416]{0:T(512)} %get-tuple-element.11.dead_col, bf16[2,30,128,192]{3,2,1,0:T(8,128)(2,1)} %get-tuple-element.7.left_hbm, bf16[2,30,192,128]{3,2,1,0:T(8,128)(2,1)} %get-tuple-element.8.right_hbm), custom_call_target="tpu_custom_call" | custom-call | flops 3000000000 | bytes 8000000 | tf_op jit(solution)/shard_map/pallas_call | solution.py:535
  273.6 1.1 slice_reduce_fusion.1
  274.7 0.1 copy.26
  274.8 0.1 stack_reshape.6
  274.9 0.1 copy.27
  275.0 0.1 stack_reshape.7
  275.2 0.1 add.60
  275.3 0.1 dynamic-slice
  275.4 0.1 reshape.90
  275.5 0.1 dynamic-slice_add_fusion
  275.6 0.1 copy.25
  275.7 0.2 fusion.2
  275.8 0.1 copy.28
  275.9 0.1 reshape.89
  276.0 0.6 and_select_fusion.1
  (12 shorter events, 0.2 us)
Async XLA Ops:
  189.9 86.1 %copy-start = (s32[2,25]{1,0:T(2,128)S(1)}, s32[2,25]{1,0:T(2,128)}, u32[]{:S(2)}) copy-start(s32[2,25]{1,0:T(2,128)} %param.23) | copy-start | bytes 604

commit v3 on v2

--- a/solution.py
+++ b/solution.py
@@ -23,6 +23,7 @@
 MICRO = 2
 ROWS = KMAX // MICRO
 CHUNK = 512
+SQ = 256
 MESH = pl.DeviceIdType.MESH
 F32 = jnp.float32
 BF16 = jnp.bfloat16
@@ -52,7 +53,7 @@
     inv_ref,
     active, pick_ref, patches, cotangent, gain, up_hbm, down_hbm,
     left_hbm, right_hbm,
-    stage_a, stage_b, w_up, w_down, xs, gs, normed, inv_std, act, hidden, pre, grad_pre,
+    stage_a, stage_b, up_0, up_1, down_0, down_1, spare, xs, gs, normed, inv_std, act, hidden, pre, grad_pre,
     left, right,
     stage_sem, left_sem, right_sem, x_send, x_recv, g_send, g_recv,
 ):
@@ -62,6 +63,8 @@
     first = section == 0
     last = section == sections - 1
     stages = (stage_a, stage_b)
+    w_up, w_down = (up_0, up_1), (down_0, down_1)
+    w_up_t, w_down_t = (down_0, down_1), (up_1, spare)
 
     def flag(l):
         return active[l:l + 1, :1] == 1
@@ -111,17 +114,13 @@
         l, kind = part // 2, part % 2
         target, cols = ((w_up, UP_COLS), (w_down, DOWN_COLS))[kind]
 
-        def place(q, carry, l=l, target=target, cols=cols, part=part):
-            rb = q // cols
-            cb = q - rb * cols
-            target[
-                l,
-                pl.ds(pl.multiple_of(rb * BLK, BLK), BLK),
-                pl.ds(pl.multiple_of(cb * BLK, BLK), BLK),
-            ] = stages[part % 2][inv_ref[part * NB + q]]
+        def place(rb, carry, l=l, target=target, cols=cols, part=part):
+            rs = pl.ds(pl.multiple_of(rb * BLK, BLK), BLK)
+            for cb in range(cols):
+                target[l][rs, cb * BLK:(cb + 1) * BLK] = stages[part % 2][inv_ref[part * NB + rb * cols + cb]]
             return carry
 
-        lax.fori_loop(0, NB, place, 0, unroll=4)
+        lax.fori_loop(0, NB // cols, place, 0)
         if part + 2 < PARTS:
             load(part + 2).start()
 
@@ -163,22 +162,22 @@
 
             def up_chunk(j, c, l=l):
                 cs = cols_of(j, CHUNK)
-                v = dot(act[l, r, :], w_up[l, :, cs])
+                v = dot(act[l, r, :], w_up[l][:, cs])
                 pre[l, r, cs] = v
                 hidden[l, r, cs] = gelu(v).astype(BF16)
                 return c
 
-            lax.fori_loop(0, FF // CHUNK, up_chunk, 0, unroll=UNROLL)
+            lax.fori_loop(0, FF // CHUNK, up_chunk, 0, unroll=True)
 
             def down_chunk(j, c, l=l):
                 cs = cols_of(j, 256)
-                v = dot(hidden[l, r, :], w_down[l, :, cs])
+                v = dot(hidden[l, r, :], w_down[l][:, cs])
                 had = xs[l, r, cs]
                 moved = (had.astype(F32) + v).astype(BF16)
                 xs[l + 1, r, cs] = jnp.where(flag(l), moved, had)
                 return c
 
-            lax.fori_loop(0, D // 256, down_chunk, 0, unroll=UNROLL)
+            lax.fori_loop(0, D // 256, down_chunk, 0, unroll=True)
 
         @pl.when(jnp.logical_not(last))
         def _():
@@ -209,6 +208,19 @@
         lax.fori_loop(0, D // BLK, turn, 0)
         save_left(l).start()
 
+    unit = (
+        lax.broadcasted_iota(jnp.int32, (SQ, SQ), 0) == lax.broadcasted_iota(jnp.int32, (SQ, SQ), 1)
+    ).astype(BF16)
+    for source, target in ((down_1, spare), (up_1, down_1), (down_0, up_1), (up_0, down_0)):
+        def flip(i, c, source=source, target=target):
+            rs = cols_of(i, SQ)
+            for j in range(source.shape[1] // SQ):
+                tile = source[rs, j * SQ:(j + 1) * SQ]
+                target[j * SQ:(j + 1) * SQ, rs] = dot_t(unit, tile).astype(BF16)
+            return c
+
+        lax.fori_loop(0, source.shape[0] // SQ, flip, 0)
+
     def save_right(l):
         return pltpu.make_async_copy(right.at[l], right_hbm.at[l], right_sem.at[l])
 
@@ -222,22 +234,22 @@
         for l in reversed(range(LMAX)):
             def hidden_chunk(j, c, l=l):
                 cs = cols_of(j, CHUNK)
-                v = dot_t(gs[l + 1, r, :], w_down[l, cs, :])
+                v = dot(gs[l + 1, r, :], w_down_t[l][:, cs])
                 p = (pre[l, r, cs] * v).astype(BF16)
                 grad_pre[l, r, cs] = p
                 for b in range(CHUNK // BLK):
                     right[l, j * (CHUNK // BLK) + b, r, :] = p[:, b * BLK:(b + 1) * BLK]
                 return c
 
-            lax.fori_loop(0, FF // CHUNK, hidden_chunk, 0, unroll=UNROLL)
+            lax.fori_loop(0, FF // CHUNK, hidden_chunk, 0, unroll=True)
 
             def act_chunk(j, c, l=l):
                 cs = cols_of(j, 256)
-                v = dot_t(grad_pre[l, r, :], w_up[l, cs, :])
+                v = dot(grad_pre[l, r, :], w_up_t[l][:, cs])
                 pre[l, r, cs] = v * gain[l:l + 1, cs]
                 return c
 
-            lax.fori_loop(0, D // 256, act_chunk, 0, unroll=UNROLL)
+            lax.fori_loop(0, D // 256, act_chunk, 0, unroll=True)
             u = pre[l, r, :D]
             n = normed[l, r, :]
             step = inv_std[l, r, :1] * (
@@ -274,9 +286,6 @@
     for l in range(LMAX):
         save_left(l).wait()
         save_right(l).wait()
-
-
-UNROLL = True
 
 
 def chain(inv, active, pick, patches, cotangent, gain, up, down):
@@ -294,8 +303,9 @@
         scratch_shapes=[
             pltpu.VMEM((NLIVE + 1, BLK, BLK), BF16),
             pltpu.VMEM((NLIVE + 1, BLK, BLK), BF16),
-            pltpu.VMEM((LMAX, D, FF), BF16),
-            pltpu.VMEM((LMAX, FF, D), BF16),
+            *[pltpu.VMEM((D, FF), BF16)] * 2,
+            *[pltpu.VMEM((FF, D), BF16)] * 2,
+            pltpu.VMEM((D, FF), BF16),
             pltpu.VMEM((LMAX + 1, KMAX, D), BF16),
             pltpu.VMEM((LMAX + 1, KMAX, D), BF16),
             pltpu.VMEM((LMAX, KMAX, D), F32),

time: 277 us -> 255 us (0.921)
  Pallas kernels: 266 us -> 244 us
    pallas_call x1, Pallas kernels: 182 us -> 157 us  [chain(): pl.pallas_call(chain_kernel, out_shape=(jax.ShapeDtypeStruct((LMAX, PANEL...]
    pallas_call x1, Pallas kernels: 83.6 us -> 87.3 us  [sums(): pl.pallas_call(sums_kernel, out_shape=jax.ShapeDtypeStruct((RING, RING, T...]
where the time goes in v3:
time: 255 us
  Pallas kernels  244 us (96%)
  local copies, waits for them, and re-layouts  5.44 us (2%)
  other arithmetic  3.81 us (1%)
    pallas_call x1, Pallas kernels, chain(): pl.pallas_call(chain_kernel, out_shape=(jax.ShapeDtypeStruct((LMAX, PANEL...  157 us
    pallas_call x1, Pallas kernels, sums(): pl.pallas_call(sums_kernel, out_shape=jax.ShapeDtypeStruct((RING, RING, T...  87.3 us

profile of v3, /device:TPU:0, one launch (start us, length us, event | category | flops | bytes accessed | tf_op | source)
XLA Modules:
  0.0 255.1 jit_solution(15234086066952557244)
XLA Ops:
  0.0 0.7 pad_add_fusion
  0.7 0.1 fusion.1
  0.9 0.2 convert_reduce_fusion
  1.1 0.3 select_reduce_fusion
  1.4 0.1 reduce_sum.40
  1.5 0.1 add.64
  1.5 0.1 add.65
  1.7 0.1 add.68
  1.8 0.7 rem.31
  2.5 0.1 rem.32
  2.6 0.7 subtract_add_fusion
  3.3 0.1 select_reduce_fusion.1
  3.5 0.7 select_n.66.inv_ref
  4.8 0.7 compare_select_fusion.1
  5.5 0.7 broadcast_in_dim.83.pick_ref
  6.9 0.7 broadcast_in_dim.81.active
  7.5 157.1 %shard_map.118 = (bf16[2,30,128,192]{3,2,1,0:T(8,128)(2,1)}, bf16[2,30,192,128]{3,2,1,0:T(8,128)(2,1)}) custom-call(s32[800]{0:T(1024)} %select_n.66.inv_ref, s32[8,128]{1,0:T(8,128)} %broadcast_in_dim.81.active, s32[192,128]{1,0:T(8,128)} %broadcast_in_dim.83.pick_ref, bf16[256,1280]{1,0:T(8,128)(2,1)} %bitcast.20, bf16[256,1280]{1,0:T(8,128)(2,1)} %bitcast.21, ...), custom_call_target="tpu_custom_call" | custom-call | flops 35000000512 | bytes 30000000 | tf_op jit(solution)/shard_map/pallas_call | solution.py:295
  164.7 87.3 %shard_map.119 = f32[4,4,32,128]{3,2,1,0:T(8,128)} custom-call(s32[416]{0:T(512)} %get-tuple-element.12.dead_row, s32[416]{0:T(512)} %get-tuple-element.11.dead_col, bf16[2,30,128,192]{3,2,1,0:T(8,128)(2,1)} %get-tuple-element.7.left_hbm, bf16[2,30,192,128]{3,2,1,0:T(8,128)(2,1)} %get-tuple-element.8.right_hbm), custom_call_target="tpu_custom_call" | custom-call | flops 3000000000 | bytes 8000000 | tf_op jit(solution)/shard_map/pallas_call | solution.py:545
  252.0 1.1 slice_reduce_fusion.1
  253.1 0.1 copy.26
  253.3 0.1 stack_reshape.6
  253.4 0.1 copy.27
  253.5 0.1 stack_reshape.7
  253.7 0.1 add.60
  253.8 0.1 dynamic-slice
  253.8 0.1 reshape.90
  253.9 0.1 dynamic-slice_add_fusion
  254.0 0.1 copy.25
  254.1 0.2 fusion.2
  254.3 0.1 copy.28
  254.4 0.1 reshape.89
  254.5 0.6 and_select_fusion.1
  (12 shorter events, 0.2 us)
Async XLA Ops:
  164.7 89.8 %copy-start = (s32[2,25]{1,0:T(2,128)S(1)}, s32[2,25]{1,0:T(2,128)}, u32[]{:S(2)}) copy-start(s32[2,25]{1,0:T(2,128)} %param.23) | copy-start | bytes 604

commit v4 on v3

--- a/solution.py
+++ b/solution.py
@@ -1,6 +1,7 @@
 import functools
 import jax
 import jax.numpy as jnp
+import numpy as np
 from jax import lax
 from jax.experimental import pallas as pl
 from jax.experimental.pallas import tpu as pltpu
@@ -18,6 +19,13 @@
 DOWN_COLS = D // BLK
 PARTS = 2 * LMAX
 PANELS = UP_COLS + DOWN_COLS
+RING = 4
+MOST = 2 * NDEAD
+FEW = 128
+HALF = BLK // 2
+TILE = 32
+OWN = 2 * NB // (RING * RING)
+WIDE = 256
 EPS_NORM = 1e-06
 EPS_SCORE = 1e-06
 MICRO = 2
@@ -51,11 +59,12 @@
 
 def chain_kernel(
     inv_ref,
-    active, pick_ref, patches, cotangent, gain, up_hbm, down_hbm,
-    left_hbm, right_hbm,
+    active, pick_ref, mask, dead, panels, patches, cotangent, gain, up_hbm, down_hbm,
+    left_hbm, right_hbm, slots_out, rank_out, wanted_out, most_out,
     stage_a, stage_b, up_0, up_1, down_0, down_1, spare, xs, gs, normed, inv_std, act, hidden, pre, grad_pre,
-    left, right,
+    left, right, row_tiles, all_tiles, most, most_up, most_down,
     stage_sem, left_sem, right_sem, x_send, x_recv, g_send, g_recv,
+    tile_send, tile_recv, all_send, all_recv, most_send, most_recv,
 ):
     sections = lax.axis_size("section")
     replica = lax.axis_index("dp")
@@ -89,13 +98,33 @@
     def _():
         pl.semaphore_signal(barrier, inc=1, device_id=(replica, section + 1), device_id_type=MESH)
 
-    @pl.when(jnp.logical_or(first, last))
-    def _():
-        pl.semaphore_wait(barrier, 1)
-
-    @pl.when(jnp.logical_not(jnp.logical_or(first, last)))
-    def _():
-        pl.semaphore_wait(barrier, 2)
+    px = replica // RING
+    py = lax.rem(replica, RING)
+
+    def along_y(step):
+        return (px * RING + lax.rem(py + step, RING), section)
+
+    def along_x(step):
+        return (lax.rem(px + step, RING) * RING + py, section)
+
+    for step in range(1, RING):
+        pl.semaphore_signal(barrier, inc=1, device_id=along_y(step), device_id_type=MESH)
+        pl.semaphore_signal(barrier, inc=1, device_id=along_x(step), device_id_type=MESH)
+
+    def moves(source, target, sends, recvs, to):
+        return [
+            pltpu.make_async_remote_copy(
+                src_ref=source, dst_ref=target, send_sem=sends.at[step - 1], recv_sem=recvs.at[step - 1],
+                device_id=to(step), device_id_type=MESH,
+            )
+            for step in range(1, RING)
+        ]
+
+    def row_moves():
+        return moves(mask, row_tiles.at[py], tile_send, tile_recv, along_y)
+
+    def all_moves():
+        return moves(row_tiles, all_tiles.at[px], all_send, all_recv, along_x)
 
     def picked(table):
         hot = pick_ref[:, :1] == lax.broadcasted_iota(jnp.int32, (KMAX, table.shape[0]), 1)
@@ -108,6 +137,65 @@
     @pl.when(last)
     def _():
         gs[LMAX] = picked(cotangent)
+
+    @pl.when(jnp.logical_or(first, last))
+    def _():
+        pl.semaphore_wait(barrier, 2 * (RING - 1) + 1)
+
+    @pl.when(jnp.logical_not(jnp.logical_or(first, last)))
+    def _():
+        pl.semaphore_wait(barrier, 2 * (RING - 1) + 2)
+
+    row_tiles[py] = mask[...]
+    for move in row_moves():
+        move.start()
+
+    def after_part(part):
+        if part == 1:
+            for move in row_moves():
+                move.wait()
+            all_tiles[px] = row_tiles[...]
+            for move in all_moves():
+                move.start()
+
+    def settle():
+        for move in all_moves():
+            move.wait()
+        count = jnp.zeros((1, 1), F32)
+        lanes = lax.broadcasted_iota(jnp.int32, (BLK, BLK), 0)
+        later = lanes < lax.broadcasted_iota(jnp.int32, (BLK, BLK), 1)
+        later = later.astype(BF16)
+        ones = jnp.ones((BLK, BLK), BF16)
+        n = RING * RING
+        under = lax.broadcasted_iota(jnp.int32, (n, n), 0) > lax.broadcasted_iota(jnp.int32, (n, n), 1)
+        spots = lax.broadcasted_iota(jnp.int32, (BLK, WIDE), 1).astype(F32)
+        for l in range(LMAX):
+            asked = all_tiles[:, :, l, :].reshape(n, BLK) * dead[l]
+            flat = asked.astype(BF16)
+            totals = dot(flat, ones)
+            rank = dot(flat, later) + dot(under.astype(BF16), totals.astype(BF16))
+            rank_out[l] = rank
+            wanted_out[l] = asked
+            count = jnp.maximum(count, jnp.sum(totals[:, :1], axis=0, keepdims=True))
+            turned = jnp.where(asked > 0.5, rank, -1.0).T
+            found = jnp.zeros((8, WIDE), F32)
+            for d in range(n):
+                hot = (turned[:, d:d + 1] == spots).astype(BF16)
+                found = found + dot(panels[d], hot)
+            slots_out[l] = found.astype(jnp.int32)
+        most[...] = jnp.broadcast_to(count, (8, BLK))
+
+    def pass_up():
+        return pltpu.make_async_remote_copy(
+            src_ref=most, dst_ref=most_up, send_sem=most_send.at[0], recv_sem=most_recv.at[0],
+            device_id=(replica, section + 1), device_id_type=MESH,
+        )
+
+    def pass_down():
+        return pltpu.make_async_remote_copy(
+            src_ref=most, dst_ref=most_down, send_sem=most_send.at[1], recv_sem=most_recv.at[1],
+            device_id=(replica, section - 1), device_id_type=MESH,
+        )
 
     for part in range(PARTS):
         load(part).wait()
@@ -121,6 +209,7 @@
             return carry
 
         lax.fori_loop(0, NB // cols, place, 0)
+        after_part(part)
         if part + 2 < PARTS:
             load(part + 2).start()
 
@@ -185,7 +274,25 @@
 
         return carry
 
+    @pl.when(jnp.logical_not(first))
+    def _():
+        settle()
+
     lax.fori_loop(0, MICRO, forward, 0)
+
+    @pl.when(first)
+    def _():
+        settle()
+
+    @pl.when(jnp.logical_not(first))
+    def _():
+        pass_up().wait_recv()
+        most[...] = jnp.maximum(most[...], most_up[...])
+
+    @pl.when(jnp.logical_not(last))
+    def _():
+        pass_up().start()
+
 
     def save_left(l):
         return pltpu.make_async_copy(left.at[l], left_hbm.at[l], left_sem.at[l])
@@ -268,6 +375,18 @@
 
     lax.fori_loop(0, MICRO, backward, 0)
 
+    @pl.when(jnp.logical_not(last))
+    def _():
+        pass_up().wait_send()
+        pass_down().wait_recv()
+        most[...] = jnp.maximum(most[...], most_down[...])
+
+    @pl.when(jnp.logical_not(first))
+    def _():
+        pass_down().start()
+
+    most_out[...] = most[...]
+
     for l in range(LMAX):
         save_right(l).start()
 
@@ -283,12 +402,17 @@
         return carry
 
     lax.fori_loop(0, MICRO, drain, 0)
+
+    @pl.when(jnp.logical_not(first))
+    def _():
+        pass_down().wait_send()
+
     for l in range(LMAX):
         save_left(l).wait()
         save_right(l).wait()
 
 
-def chain(inv, active, pick, patches, cotangent, gain, up, down):
+def chain(inv, active, pick, mask, dead, panels, patches, cotangent, gain, up, down):
     smem = pl.BlockSpec(memory_space=pltpu.SMEM)
     vmem = pl.BlockSpec(memory_space=pltpu.VMEM)
     hbm = pl.BlockSpec(memory_space=pl.ANY)
@@ -297,9 +421,13 @@
         out_shape=(
             jax.ShapeDtypeStruct((LMAX, PANELS, BLK, KMAX), BF16),
             jax.ShapeDtypeStruct((LMAX, PANELS, KMAX, BLK), BF16),
+            jax.ShapeDtypeStruct((LMAX, 8, WIDE), jnp.int32),
+            jax.ShapeDtypeStruct((LMAX, RING * RING, BLK), F32),
+            jax.ShapeDtypeStruct((LMAX, RING * RING, BLK), F32),
+            jax.ShapeDtypeStruct((8, BLK), F32),
         ),
-        in_specs=[smem] + [vmem] * 5 + [hbm] * 2,
-        out_specs=(hbm, hbm),
+        in_specs=[smem] + [vmem] * 8 + [hbm] * 2,
+        out_specs=(hbm, hbm, vmem, vmem, vmem, vmem),
         scratch_shapes=[
             pltpu.VMEM((NLIVE + 1, BLK, BLK), BF16),
             pltpu.VMEM((NLIVE + 1, BLK, BLK), BF16),
@@ -316,6 +444,9 @@
             pltpu.VMEM((LMAX, KMAX, FF), BF16),
             pltpu.VMEM((LMAX, PANELS, BLK, KMAX), BF16),
             pltpu.VMEM((LMAX, PANELS, KMAX, BLK), BF16),
+            pltpu.VMEM((RING, 8, BLK), F32),
+            pltpu.VMEM((RING, RING, 8, BLK), F32),
+            *[pltpu.VMEM((8, BLK), F32)] * 3,
             pltpu.SemaphoreType.DMA((PARTS,)),
             pltpu.SemaphoreType.DMA((LMAX,)),
             pltpu.SemaphoreType.DMA((LMAX,)),
@@ -323,42 +454,26 @@
             pltpu.SemaphoreType.DMA((MICRO,)),
             pltpu.SemaphoreType.DMA((MICRO,)),
             pltpu.SemaphoreType.DMA((MICRO,)),
+            *[pltpu.SemaphoreType.DMA((RING - 1,))] * 4,
+            *[pltpu.SemaphoreType.DMA((2,))] * 2,
         ],
         compiler_params=pltpu.CompilerParams(
             collective_id=0, has_side_effects=True, vmem_limit_bytes=60 * 1024 * 1024
         ),
         cost_estimate=pl.CostEstimate(flops=35_000_000_000, bytes_accessed=30_000_000, transcendentals=2_000_000),
-    )(inv, active, pick, patches, cotangent, gain, up, down)
-
-
-def tables(up_index, down_index):
+    )(inv, active, pick, mask, dead, panels, patches, cotangent, gain, up, down)
+
+
+def live_tables(up_index, down_index):
     listed = jnp.stack([up_index, down_index], axis=1).reshape(PARTS, NLIVE)
     hit = listed[:, :, None] == jnp.arange(NB)[None, None, :]
     live = jnp.any(hit, axis=1)
     inv = jnp.where(live, jnp.sum(jnp.where(hit, jnp.arange(NLIVE)[None, :, None], 0), axis=1), NLIVE)
-    q = jnp.arange(NB)
-    dead = jnp.logical_not(live)
-    rank = jnp.sum((dead[:, :, None] & (q[:, None] < q[None, :])[None]).astype(jnp.int32), axis=1)
-    k = jnp.arange(NDEAD)
-    at = dead[:, None, :] & (rank[:, None, :] == k[None, :, None])
-    number = jnp.sum(jnp.where(at, q[None, None, :], 0), axis=2)
-    cols = jnp.array([UP_COLS, DOWN_COLS] * LMAX)[:, None]
-    row = number // cols
-    col = number - row * cols
-    base = jnp.arange(PARTS)[:, None] % 2
-    row = (row + base * DOWN_COLS).astype(jnp.int32)
-    col = (col + base * UP_COLS).astype(jnp.int32)
-    return inv.astype(jnp.int32), live, rank, row, col
-
-
-RING = 4
-PER = 2 * NDEAD // (RING * RING)
-HALF = BLK // 2
-TILE = 32
+    return inv.astype(jnp.int32), live.reshape(LMAX, 2 * NB)
 
 
 def sums_kernel(
-    dead_row, dead_col, left_hbm, right_hbm, out_ref,
+    PER, slots, left_hbm, right_hbm, out_ref,
     left_0, left_1, right_0, right_1,
     opp_0, opp_1, nxt_0, nxt_1, prv_0, prv_1, mid_0, mid_1,
     ra_0, ra_1, rb_0, rb_1, ia_0, ia_1, ib_0, ib_1,
@@ -407,8 +522,8 @@
         return lax.rem(place[axis] + step, RING)
 
     def block(h, f, c, g):
-        where = (LMAX - 1 - h) * 2 * NDEAD + (f * PER + c) * RING + g
-        return dot(lefts[h][dead_row[where]], rights[h][dead_col[where]])
+        l, s = LMAX - 1 - h, (f * PER + c) * RING + g
+        return dot(lefts[h][slots[l, 0, s]], rights[h][slots[l, 1, s]])
 
     def send(h, kind, c, src, dst, axis, step):
         return pltpu.make_async_remote_copy(
@@ -535,7 +650,8 @@
     lax.fori_loop(0, PER, drain, 0)
 
 
-def sums(dead_row, dead_col, left, right):
+def sums(size, number, slots, left, right):
+    PER = size // (RING * RING)
     smem = pl.BlockSpec(memory_space=pltpu.SMEM)
     hbm = pl.BlockSpec(memory_space=pl.ANY)
 
@@ -543,9 +659,9 @@
         return [pltpu.VMEM((PER, *lead, BLK), BF16)] * 2
 
     return pl.pallas_call(
-        sums_kernel,
+        functools.partial(sums_kernel, PER),
         out_shape=jax.ShapeDtypeStruct((RING, RING, TILE, BLK), F32),
-        in_specs=[smem] * 2 + [hbm] * 2,
+        in_specs=[smem] + [hbm] * 2,
         out_specs=pl.BlockSpec(memory_space=pltpu.VMEM),
         scratch_shapes=[
             *[pltpu.VMEM((PANELS, BLK, KMAX), BF16)] * 2,
@@ -563,34 +679,59 @@
             *[pltpu.SemaphoreType.DMA((RING - 1,))] * 4,
         ],
         compiler_params=pltpu.CompilerParams(
-            collective_id=1, has_side_effects=True, vmem_limit_bytes=60 * 1024 * 1024
+            collective_id=number, has_side_effects=True, vmem_limit_bytes=60 * 1024 * 1024
         ),
         cost_estimate=pl.CostEstimate(flops=3_000_000_000, bytes_accessed=8_000_000, transcendentals=0),
-    )(dead_row, dead_col, left, right)
+    )(slots, left, right)
+
+
+def every_score(size, number, slots, left, right):
+    per = size // (RING * RING)
+    tiles = sums(size, number, slots, left, right)
+    half = TILE // 2
+    late = tiles[:, :, :per, 0].transpose(1, 2, 0).reshape(size)
+    early = tiles[:, :, half:half + per, 0].transpose(0, 2, 1).reshape(size)
+    return jnp.pad(jnp.stack([early, late]), ((0, 0), (0, MOST - size)))
+
+
+def panel_numbers():
+    q = np.arange(2 * NB)
+    lower = q >= NB
+    inner = np.where(lower, q - NB, q)
+    cols = np.where(lower, DOWN_COLS, UP_COLS)
+    row = np.where(lower, inner // cols + DOWN_COLS, inner // cols)
+    col = np.where(lower, inner % cols + UP_COLS, inner % cols)
+    table = np.zeros((RING * RING, 8, BLK), np.float32)
+    table[:, 0, :OWN] = row.reshape(-1, OWN)
+    table[:, 1, :OWN] = col.reshape(-1, OWN)
+    return jnp.asarray(table, BF16)
 
 
 def body(patches, cotangent, keep_order, keep_count, destination, norm_gain, up_blocks, up_index,
          down_blocks, down_index, layer_count, regrow_mask):
-    replicas = lax.axis_size("dp")
     replica_id = lax.axis_index("dp")
-    inv, live, rank, row, col = tables(up_index, down_index)
+    inv, live = live_tables(up_index, down_index)
+    dead = jnp.logical_not(live).reshape(LMAX, RING * RING, OWN)
+    dead = jnp.pad(dead.astype(F32), ((0, 0), (0, 0), (0, BLK - OWN)))
+    mask = jnp.pad((regrow_mask == 1).astype(F32), ((0, 8 - LMAX), (0, BLK - OWN)))
     kept = jnp.where(jnp.arange(KMAX) < keep_count[0], keep_order[0, :KMAX], -1)
     pick = jnp.broadcast_to(kept[:, None], (KMAX, BLK)).astype(jnp.int32)
     active = jnp.broadcast_to((jnp.arange(8) < layer_count[0])[:, None], (8, BLK)).astype(jnp.int32)
-    left, right = chain(inv.reshape(-1), active, pick, patches[0], cotangent[0], norm_gain, up_blocks, down_blocks)
-    tiles = sums(row.reshape(-1), col.reshape(-1), left, right)
-    half = TILE // 2
-    late = tiles[:, :, :PER, 0].transpose(1, 2, 0).reshape(2 * NDEAD)
-    early = tiles[:, :, half:half + PER, 0].transpose(0, 2, 1).reshape(2 * NDEAD)
-    every = jnp.stack([early, late])
-    share = 2 * NB // replicas
-    start = replica_id * share
-    slot = rank.reshape(LMAX, 2, NB) + (jnp.arange(2) * NDEAD)[None, :, None]
-    slot = lax.dynamic_slice_in_dim(slot.reshape(LMAX, 2 * NB), start, share, 1)
-    alive = lax.dynamic_slice_in_dim(live.reshape(LMAX, 2 * NB), start, share, 1)
-    picked = jnp.sum(jnp.where(slot[:, :, None] == jnp.arange(2 * NDEAD), every[:, None, :], 0.0), axis=2)
-    eligible = jnp.logical_and(jnp.logical_not(alive), regrow_mask == 1)
-    return jnp.where(eligible, picked, 0.0)
+    left, right, slots, rank, wanted, most = chain(
+        inv.reshape(-1), active, pick, mask, dead, panel_numbers(), patches[0], cotangent[0], norm_gain,
+        up_blocks, down_blocks,
+    )
+    every = lax.cond(
+        most[0, 0] < FEW + 0.5,
+        functools.partial(every_score, FEW, 1),
+        functools.partial(every_score, MOST, 2),
+        slots, left, right,
+    )
+    rank = lax.dynamic_index_in_dim(rank, replica_id, 1, keepdims=False)[:, :OWN]
+    wanted = lax.dynamic_index_in_dim(wanted, replica_id, 1, keepdims=False)[:, :OWN]
+    spots = jnp.arange(MOST).astype(F32)
+    picked = jnp.sum(jnp.where(rank[:, :, None] == spots, every[:, None, :], 0.0), axis=2)
+    return jnp.where(wanted > 0.5, picked, 0.0)
 
 
 def solution(mesh):

time: 255 us -> 231 us (0.906)
  Pallas kernels: 244 us -> 218 us
    pallas_call x1, Pallas kernels: 87.3 us -> 57.9 us  [sums(): pl.pallas_call(functools.partial(sums_kernel, PER), out_shape=jax.ShapeDt...]
    pallas_call x1, Pallas kernels: 157 us -> 161 us  [chain(): pl.pallas_call(chain_kernel, out_shape=(jax.ShapeDtypeStruct((LMAX, PANEL...]
where the time goes in v4:
time: 231 us; the launch traced here: 230 us
  Pallas kernels  218 us (94%)
  local copies, waits for them, and re-layouts  6.29 us (3%)
  other arithmetic  3.75 us (2%)
    pallas_call x1, Pallas kernels, chain(): pl.pallas_call(chain_kernel, out_shape=(jax.ShapeDtypeStruct((LMAX, PANEL...  161 us
    pallas_call x1, Pallas kernels, sums(): pl.pallas_call(functools.partial(sums_kernel, PER), out_shape=jax.ShapeDt...  57.9 us

profile of v4, /device:TPU:0, one launch (start us, length us, event | category | flops | bytes accessed | tf_op | source)
XLA Modules:
  0.0 230.5 jit_solution(8192976883436069484)
XLA Ops:
  1.3 0.7 compare_select_fusion.2
  2.0 0.7 broadcast_compare_fusion
  2.7 0.7 pad_add_fusion
  3.4 0.1 fusion
  3.5 0.1 select_reduce_fusion
  3.7 0.7 select_n.35.inv_ref
  4.4 0.1 convert_element_type.28
  4.4 0.6 pad_convert_fusion.1.mask
  5.0 0.7 broadcast_in_dim.56.active
  5.7 0.6 pad_convert_fusion.dead
  6.3 0.7 broadcast_in_dim.58.pick_ref
  7.0 160.5 %shard_map.118 = (bf16[2,30,128,192]{3,2,1,0:T(8,128)(2,1)}, bf16[2,30,192,128]{3,2,1,0:T(8,128)(2,1)S(1)}, s32[2,8,256]{2,1,0:T(8,128)S(1)}, f32[2,16,128]{2,1,...) custom-call(s32[800]{0:T(1024)} %select_n.35.inv_ref, s32[8,128]{1,0:T(8,128)} %broadcast_in_dim.56.active, ...), custom_call_target="tpu_custom_call" | custom-call | flops 35000000512 | bytes 30000000 | tf_op jit(solution)/shard_map/pallas_call | solution.py:419
  167.6 1.2 slice.27
  169.4 0.7 constant_dynamic-slice_fusion
  170.1 59.3 %conditional.1 = (f32[2,208]{1,0:T(2,128)S(1)}) conditional(s32[]{:T(128)} %bitcast.14, (s32[2,8,256]{2,1,0:T(8,128)S(1)}, bf16[2,30,128,192]{3,2,1,0:T(8,128)(2,1)}, bf16[2,30,192,128]{3,2,1,0:T(8,128)(2,1)S(1)}) %tuple.11, (s32[2,8,256]{2,1,0:T(8,128)S(1)}, bf16[2,30,128,192]{3,2,1,0:T(8,128)(2,1)}, bf16[2,30,192,128]{3,2,1,0:T(8,128)(2,1)S(1)}) %tuple.11), branch_computations={%region_2.3_spmd, %region_3.4_spmd} | conditional | flops 3000001536 | bytes 8013320 | solution.py:724
  170.1 57.9 %branch_1_fun.1 = f32[4,4,32,128]{3,2,1,0:T(8,128)} custom-call(s32[2,8,256]{2,1,0:T(8,128)S(1)} %get-tuple-element.23.slots, bf16[2,30,128,192]{3,2,1,0:T(8,128)(2,1)} %get-tuple-element.24.left_hbm, bf16[2,30,192,128]{3,2,1,0:T(8,128)(2,1)S(1)} %get-tuple-element.25.right_hbm), custom_call_target="tpu_custom_call" | custom-call | flops 3000000000 | bytes 8000000 | tf_op jit(solution)/shard_map/cond/branch_1_fun/pallas_call | solution.py:661
  228.0 1.0 slice_reduce_fusion.3
  229.0 0.1 copy.29
  229.1 0.1 reshape.46
  229.2 0.1 copy.28
  229.3 0.1 reshape.45
  229.5 0.1 copy.34
  229.6 0.1 copy.32
  229.7 0.2 fusion.1
  229.9 0.6 copy.33
  (7 shorter events, 0.0 us)

commit v5 on v4

--- a/solution.py
+++ b/solution.py
@@ -32,6 +32,7 @@
 ROWS = KMAX // MICRO
 CHUNK = 512
 SQ = 256
+FLIP = 5
 MESH = pl.DeviceIdType.MESH
 F32 = jnp.float32
 BF16 = jnp.bfloat16
@@ -59,10 +60,10 @@
 
 def chain_kernel(
     inv_ref,
-    active, pick_ref, mask, dead, panels, patches, cotangent, gain, up_hbm, down_hbm,
-    left_hbm, right_hbm, slots_out, rank_out, wanted_out, most_out,
+    count_ref, order, kept, asked_ref, dead, panels, patches, cotangent, gain, up_hbm, down_hbm,
+    left_hbm, right_hbm, slots_out, own_out, most_out,
     stage_a, stage_b, up_0, up_1, down_0, down_1, spare, xs, gs, normed, inv_std, act, hidden, pre, grad_pre,
-    left, right, row_tiles, all_tiles, most, most_up, most_down,
+    left, right, mask, row_tiles, all_tiles, most, most_up, most_down,
     stage_sem, left_sem, right_sem, x_send, x_recv, g_send, g_recv,
     tile_send, tile_recv, all_send, all_recv, most_send, most_recv,
 ):
@@ -76,7 +77,7 @@
     w_up_t, w_down_t = (down_0, down_1), (up_1, spare)
 
     def flag(l):
-        return active[l:l + 1, :1] == 1
+        return count_ref[:, :] > l
 
     def load(part):
         l, kind = part // 2, part % 2
@@ -127,8 +128,14 @@
         return moves(row_tiles, all_tiles.at[px], all_send, all_recv, along_x)
 
     def picked(table):
-        hot = pick_ref[:, :1] == lax.broadcasted_iota(jnp.int32, (KMAX, table.shape[0]), 1)
-        return dot(hot.astype(BF16), table[...]).astype(BF16)
+        size = table.shape[0]
+        hot = jnp.logical_and(
+            lax.broadcasted_iota(jnp.int32, (size, KMAX), 0) == order[:, :KMAX],
+            lax.broadcasted_iota(jnp.int32, (size, KMAX), 1) < kept[:, :],
+        )
+        return lax.dot_general(
+            hot.astype(BF16), table[...], (((0,), (0,)), ((), ())), preferred_element_type=F32
+        ).astype(BF16)
 
     @pl.when(first)
     def _():
@@ -146,6 +153,8 @@
     def _():
         pl.semaphore_wait(barrier, 2 * (RING - 1) + 2)
 
+    mask[...] = jnp.zeros((8, BLK), F32)
+    mask[:LMAX, :OWN] = (asked_ref[...] == 1).astype(F32)
     row_tiles[py] = mask[...]
     for move in row_moves():
         move.start()
@@ -174,8 +183,9 @@
             flat = asked.astype(BF16)
             totals = dot(flat, ones)
             rank = dot(flat, later) + dot(under.astype(BF16), totals.astype(BF16))
-            rank_out[l] = rank
-            wanted_out[l] = asked
+            mine = lax.broadcasted_iota(jnp.int32, (n, BLK), 0) == replica
+            own_out[l:l + 1, :] = jnp.sum(jnp.where(mine, rank, 0.0), axis=0, keepdims=True)
+            own_out[LMAX + l:LMAX + l + 1, :] = jnp.sum(jnp.where(mine, asked, 0.0), axis=0, keepdims=True)
             count = jnp.maximum(count, jnp.sum(totals[:, :1], axis=0, keepdims=True))
             turned = jnp.where(asked > 0.5, rank, -1.0).T
             found = jnp.zeros((8, WIDE), F32)
@@ -297,36 +307,28 @@
     def save_left(l):
         return pltpu.make_async_copy(left.at[l], left_hbm.at[l], left_sem.at[l])
 
-    for l in range(LMAX):
-        def slopes(j, c, l=l):
-            cs = cols_of(j, BLK)
-            pre[l, :, cs] = gelu_slope(pre[l, :, cs])
-            h = jnp.where(flag(l), hidden[l, :, cs], jnp.zeros((KMAX, BLK), BF16))
-            left[l, DOWN_COLS + j] = h.T
-            return c
-
-        lax.fori_loop(0, FF // BLK, slopes, 0)
-
-        def turn(j, c, l=l):
-            a = jnp.where(flag(l), act[l, :, cols_of(j, BLK)], jnp.zeros((KMAX, BLK), BF16))
-            left[l, j] = a.T
-            return c
-
-        lax.fori_loop(0, D // BLK, turn, 0)
-        save_left(l).start()
-
-    unit = (
-        lax.broadcasted_iota(jnp.int32, (SQ, SQ), 0) == lax.broadcasted_iota(jnp.int32, (SQ, SQ), 1)
-    ).astype(BF16)
+    def keep_left():
+        for l in range(LMAX):
+            for j in range(UP_COLS):
+                h = jnp.where(flag(l), hidden[l, :, j * BLK:(j + 1) * BLK], jnp.zeros((KMAX, BLK), BF16))
+                left[l, DOWN_COLS + j] = h.T
+            for j in range(DOWN_COLS):
+                a = jnp.where(flag(l), act[l, :, j * BLK:(j + 1) * BLK], jnp.zeros((KMAX, BLK), BF16))
+                left[l, j] = a.T
+            save_left(l).start()
+
+    @pl.when(jnp.logical_not(last))
+    def _():
+        keep_left()
+
     for source, target in ((down_1, spare), (up_1, down_1), (down_0, up_1), (up_0, down_0)):
         def flip(i, c, source=source, target=target):
             rs = cols_of(i, SQ)
             for j in range(source.shape[1] // SQ):
-                tile = source[rs, j * SQ:(j + 1) * SQ]
-                target[j * SQ:(j + 1) * SQ, rs] = dot_t(unit, tile).astype(BF16)
+                target[j * SQ:(j + 1) * SQ, rs] = source[rs, j * SQ:(j + 1) * SQ].T
             return c
 
-        lax.fori_loop(0, source.shape[0] // SQ, flip, 0)
+        lax.fori_loop(0, source.shape[0] // SQ, flip, 0, unroll=FLIP)
 
     def save_right(l):
         return pltpu.make_async_copy(right.at[l], right_hbm.at[l], right_sem.at[l])
@@ -342,7 +344,7 @@
             def hidden_chunk(j, c, l=l):
                 cs = cols_of(j, CHUNK)
                 v = dot(gs[l + 1, r, :], w_down_t[l][:, cs])
-                p = (pre[l, r, cs] * v).astype(BF16)
+                p = (gelu_slope(pre[l, r, cs]) * v).astype(BF16)
                 grad_pre[l, r, cs] = p
                 for b in range(CHUNK // BLK):
                     right[l, j * (CHUNK // BLK) + b, r, :] = p[:, b * BLK:(b + 1) * BLK]
@@ -390,6 +392,10 @@
     for l in range(LMAX):
         save_right(l).start()
 
+    @pl.when(last)
+    def _():
+        keep_left()
+
     def drain(mb, carry):
         @pl.when(jnp.logical_not(last))
         def _():
@@ -412,7 +418,7 @@
         save_right(l).wait()
 
 
-def chain(inv, active, pick, mask, dead, panels, patches, cotangent, gain, up, down):
+def chain(inv, count, order, kept, asked, dead, panels, patches, cotangent, gain, up, down):
     smem = pl.BlockSpec(memory_space=pltpu.SMEM)
     vmem = pl.BlockSpec(memory_space=pltpu.VMEM)
     hbm = pl.BlockSpec(memory_space=pl.ANY)
@@ -422,12 +428,11 @@
             jax.ShapeDtypeStruct((LMAX, PANELS, BLK, KMAX), BF16),
             jax.ShapeDtypeStruct((LMAX, PANELS, KMAX, BLK), BF16),
             jax.ShapeDtypeStruct((LMAX, 8, WIDE), jnp.int32),
-            jax.ShapeDtypeStruct((LMAX, RING * RING, BLK), F32),
-            jax.ShapeDtypeStruct((LMAX, RING * RING, BLK), F32),
+            jax.ShapeDtypeStruct((2 * LMAX, BLK), F32),
             jax.ShapeDtypeStruct((8, BLK), F32),
         ),
-        in_specs=[smem] + [vmem] * 8 + [hbm] * 2,
-        out_specs=(hbm, hbm, vmem, vmem, vmem, vmem),
+        in_specs=[smem] + [vmem] * 9 + [hbm] * 2,
+        out_specs=(hbm, hbm, vmem, vmem, vmem),
         scratch_shapes=[
             pltpu.VMEM((NLIVE + 1, BLK, BLK), BF16),
             pltpu.VMEM((NLIVE + 1, BLK, BLK), BF16),
@@ -444,6 +449,7 @@
             pltpu.VMEM((LMAX, KMAX, FF), BF16),
             pltpu.VMEM((LMAX, PANELS, BLK, KMAX), BF16),
             pltpu.VMEM((LMAX, PANELS, KMAX, BLK), BF16),
+            pltpu.VMEM((8, BLK), F32),
             pltpu.VMEM((RING, 8, BLK), F32),
             pltpu.VMEM((RING, RING, 8, BLK), F32),
             *[pltpu.VMEM((8, BLK), F32)] * 3,
@@ -461,7 +467,7 @@
             collective_id=0, has_side_effects=True, vmem_limit_bytes=60 * 1024 * 1024
         ),
         cost_estimate=pl.CostEstimate(flops=35_000_000_000, bytes_accessed=30_000_000, transcendentals=2_000_000),
-    )(inv, active, pick, mask, dead, panels, patches, cotangent, gain, up, down)
+    )(inv, count, order, kept, asked, dead, panels, patches, cotangent, gain, up, down)
 
 
 def live_tables(up_index, down_index):
@@ -478,8 +484,8 @@
     opp_0, opp_1, nxt_0, nxt_1, prv_0, prv_1, mid_0, mid_1,
     ra_0, ra_1, rb_0, rb_1, ia_0, ia_1, ib_0, ib_1,
     sa_0, sa_1, sb_0, sb_1, ja_0, ja_1, jb_0, jb_1,
-    squares, mine, row_tiles, all_tiles,
-    load_sem, send_sem, recv_sem, tile_send, tile_recv, full_send, full_recv,
+    squares, mine, all_tiles,
+    load_sem, send_sem, recv_sem, tile_send, tile_recv,
 ):
     section = lax.axis_index("section")
     replica = lax.axis_index("dp")
@@ -505,10 +511,14 @@
             copy.start()
 
     barrier = pltpu.get_barrier_semaphore()
-    for axis in range(2):
-        for step in range(1, RING):
-            pl.semaphore_signal(barrier, inc=1, device_id=peer(axis, step), device_id_type=MESH)
-    pl.semaphore_wait(barrier, 2 * (RING - 1))
+    everyone = RING * RING
+
+    def other(step):
+        return (lax.rem(replica + step, everyone), section)
+
+    for step in range(1, everyone):
+        pl.semaphore_signal(barrier, inc=1, device_id=other(step), device_id_type=MESH)
+    pl.semaphore_wait(barrier, everyone - 1)
     for h in range(2):
         for copy in load(h):
             copy.wait()
@@ -622,30 +632,18 @@
     mean = jnp.sum(squares[...].reshape(TILE, BLK), axis=1, keepdims=True) * (1.0 / (BLK * BLK))
     mine[...] = jnp.broadcast_to(jnp.sqrt(mean / rows_total + EPS_SCORE), (TILE, BLK))
 
-    row_tiles[px] = mine[...]
-    rows = [
-        pltpu.make_async_remote_copy(
-            src_ref=mine, dst_ref=row_tiles.at[px], send_sem=tile_send.at[step - 1],
-            recv_sem=tile_recv.at[step - 1], device_id=peer(0, step), device_id_type=MESH,
-        )
-        for step in range(1, RING)
-    ]
-    for move in rows:
-        move.start()
-    for move in rows:
-        move.wait()
-    all_tiles[py] = row_tiles[...]
-    cols = [
-        pltpu.make_async_remote_copy(
-            src_ref=row_tiles, dst_ref=all_tiles.at[py], send_sem=full_send.at[step - 1],
-            recv_sem=full_recv.at[step - 1], device_id=peer(1, step), device_id_type=MESH,
-        )
-        for step in range(1, RING)
-    ]
-    for move in cols:
-        move.start()
-    for move in cols:
-        move.wait()
+    all_tiles[replica] = mine[...]
+
+    def tile(step):
+        return pltpu.make_async_remote_copy(
+            src_ref=mine, dst_ref=all_tiles.at[replica], send_sem=tile_send.at[step - 1],
+            recv_sem=tile_recv.at[step - 1], device_id=other(step), device_id_type=MESH,
+        )
+
+    for step in range(1, everyone):
+        tile(step).start()
+    for step in range(1, everyone):
+        tile(step).wait()
     out_ref[...] = all_tiles[...]
     lax.fori_loop(0, PER, drain, 0)
 
@@ -660,7 +658,7 @@
 
     return pl.pallas_call(
         functools.partial(sums_kernel, PER),
-        out_shape=jax.ShapeDtypeStruct((RING, RING, TILE, BLK), F32),
+        out_shape=jax.ShapeDtypeStruct((RING * RING, TILE, BLK), F32),
         in_specs=[smem] + [hbm] * 2,
         out_specs=pl.BlockSpec(memory_space=pltpu.VMEM),
         scratch_shapes=[
@@ -671,12 +669,11 @@
             *blocks(HALF), *blocks(HALF), *blocks(BLK), *blocks(BLK),
             pltpu.VMEM((2, TILE // 2, BLK), F32),
             pltpu.VMEM((TILE, BLK), F32),
-            pltpu.VMEM((RING, TILE, BLK), F32),
-            pltpu.VMEM((RING, RING, TILE, BLK), F32),
+            pltpu.VMEM((RING * RING, TILE, BLK), F32),
             pltpu.SemaphoreType.DMA((2, 2)),
             pltpu.SemaphoreType.DMA((2, 8, PER)),
             pltpu.SemaphoreType.DMA((2, 8, PER)),
-            *[pltpu.SemaphoreType.DMA((RING - 1,))] * 4,
+            *[pltpu.SemaphoreType.DMA((RING * RING - 1,))] * 2,
         ],
         compiler_params=pltpu.CompilerParams(
             collective_id=number, has_side_effects=True, vmem_limit_bytes=60 * 1024 * 1024
@@ -689,8 +686,9 @@
     per = size // (RING * RING)
     tiles = sums(size, number, slots, left, right)
     half = TILE // 2
-    late = tiles[:, :, :per, 0].transpose(1, 2, 0).reshape(size)
-    early = tiles[:, :, half:half + per, 0].transpose(0, 2, 1).reshape(size)
+    tiles = tiles[:, :, 0].reshape(RING, RING, TILE)
+    late = tiles[:, :, :per].transpose(0, 2, 1).reshape(size)
+    early = tiles[:, :, half:half + per].transpose(1, 2, 0).reshape(size)
     return jnp.pad(jnp.stack([early, late]), ((0, 0), (0, MOST - size)))
 
 
@@ -709,16 +707,12 @@
 
 def body(patches, cotangent, keep_order, keep_count, destination, norm_gain, up_blocks, up_index,
          down_blocks, down_index, layer_count, regrow_mask):
-    replica_id = lax.axis_index("dp")
     inv, live = live_tables(up_index, down_index)
     dead = jnp.logical_not(live).reshape(LMAX, RING * RING, OWN)
     dead = jnp.pad(dead.astype(F32), ((0, 0), (0, 0), (0, BLK - OWN)))
-    mask = jnp.pad((regrow_mask == 1).astype(F32), ((0, 8 - LMAX), (0, BLK - OWN)))
-    kept = jnp.where(jnp.arange(KMAX) < keep_count[0], keep_order[0, :KMAX], -1)
-    pick = jnp.broadcast_to(kept[:, None], (KMAX, BLK)).astype(jnp.int32)
-    active = jnp.broadcast_to((jnp.arange(8) < layer_count[0])[:, None], (8, BLK)).astype(jnp.int32)
-    left, right, slots, rank, wanted, most = chain(
-        inv.reshape(-1), active, pick, mask, dead, panel_numbers(), patches[0], cotangent[0], norm_gain,
+    left, right, slots, own, most = chain(
+        inv.reshape(-1), layer_count.reshape(1, 1), keep_order, keep_count.reshape(1, 1), regrow_mask, dead,
+        panel_numbers(), patches[0], cotangent[0], norm_gain,
         up_blocks, down_blocks,
     )
     every = lax.cond(
@@ -727,8 +721,7 @@
         functools.partial(every_score, MOST, 2),
         slots, left, right,
     )
-    rank = lax.dynamic_index_in_dim(rank, replica_id, 1, keepdims=False)[:, :OWN]
-    wanted = lax.dynamic_index_in_dim(wanted, replica_id, 1, keepdims=False)[:, :OWN]
+    rank, wanted = own[:LMAX, :OWN], own[LMAX:, :OWN]
     spots = jnp.arange(MOST).astype(F32)
     picked = jnp.sum(jnp.where(rank[:, :, None] == spots, every[:, None, :], 0.0), axis=2)
     return jnp.where(wanted > 0.5, picked, 0.0)

time: 231 us -> 212 us (0.918)
  Pallas kernels: 218 us -> 203 us
  local copies, waits for them, and re-layouts: 6.29 us -> 3.73 us
    pallas_call x1, Pallas kernels: 161 us -> 147 us  [chain(): pl.pallas_call(chain_kernel, out_shape=(jax.ShapeDtypeStruct((LMAX, PANEL...]
where the time goes in v5:
time: 212 us; the launch traced here: 211 us
  Pallas kernels  203 us (96%)
  local copies, waits for them, and re-layouts  3.73 us (2%)
  other arithmetic  2.34 us (1%)
    pallas_call x1, Pallas kernels, chain(): pl.pallas_call(chain_kernel, out_shape=(jax.ShapeDtypeStruct((LMAX, PANEL...  147 us
    pallas_call x1, Pallas kernels, sums(): pl.pallas_call(functools.partial(sums_kernel, PER), out_shape=jax.ShapeDt...  55.8 us

profile of v5, /device:TPU:0, one launch (start us, length us, event | category | flops | bytes accessed | tf_op | source)
XLA Modules:
  0.0 211.3 jit_solution(8880528621771067781)
XLA Ops:
  0.0 0.7 pad_add_fusion
  0.7 0.1 fusion
  0.8 0.1 select_reduce_fusion
  1.0 0.7 select_n.22.inv_ref
  1.7 0.1 convert_element_type.21
  1.8 0.6 pad_convert_fusion.dead
  3.7 147.2 %shard_map.118 = (bf16[2,30,128,192]{3,2,1,0:T(8,128)(2,1)}, bf16[2,30,192,128]{3,2,1,0:T(8,128)(2,1)S(1)}, s32[2,8,256]{2,1,0:T(8,128)S(1)}, f32[4,128]{1,0:T(4,128)}, f32[8,128]{1,0:T(8,128)}) custom-call(s32[800]{0:T(1024)} %select_n.22.inv_ref, s32[1,1]{1,0:T(1,128)} %bitcast.19.count_ref, s32[1,256]{1,0:T(1,128)} %order.1, s32[1,1]{1,0:T(1,128)} %bitcast.18.kept, ...), custom_call_target="tpu_custom_call" | custom-call | flops 35000000512 | bytes 30000000 | tf_op jit(solution)/shard_map/pallas_call | solution.py:425
  150.9 1.2 slice.29
  152.7 0.0 copy-start
  152.7 57.6 %conditional.1 = (f32[2,208]{1,0:T(2,128)S(1)}) conditional(s32[]{:T(128)} %bitcast.11, (s32[2,8,256]{2,1,0:T(8,128)S(1)}, bf16[2,30,128,192]{3,2,1,0:T(8,128)(2,1)}, bf16[2,30,192,128]{3,2,1,0:T(8,128)(2,1)S(1)}) %tuple.11, (s32[2,8,256]{2,1,0:T(8,128)S(1)}, bf16[2,30,128,192]{3,2,1,0:T(8,128)(2,1)}, bf16[2,30,192,128]{3,2,1,0:T(8,128)(2,1)S(1)}) %tuple.11), branch_computations={%region_2.3_spmd, %region_3.4_spmd} | conditional | flops 3000001536 | bytes 8017416 | solution.py:718
  153.0 55.8 %branch_1_fun.1 = f32[16,32,128]{2,1,0:T(8,128)} custom-call(s32[2,8,256]{2,1,0:T(8,128)S(1)} %get-tuple-element.23.slots, bf16[2,30,128,192]{3,2,1,0:T(8,128)(2,1)} %get-tuple-element.24.left_hbm, bf16[2,30,192,128]{3,2,1,0:T(8,128)(2,1)S(1)} %get-tuple-element.25.right_hbm), custom_call_target="tpu_custom_call" | custom-call | flops 3000000000 | bytes 8000000 | tf_op jit(solution)/shard_map/cond/branch_1_fun/pallas_call | solution.py:659
  208.8 1.1 slice_reduce_fusion.1
  209.9 0.1 slice_bitcast_fusion.3
  209.9 0.1 copy.24
  210.0 0.1 reshape.36
  210.1 0.1 copy.25
  210.2 0.1 reshape.37
  210.4 0.0 copy-done
  210.4 0.1 copy.27
  210.5 0.2 fusion.1
  210.7 0.1 copy.28
  210.8 0.6 compare_select_fusion.1
  (6 shorter events, 0.0 us)
Async XLA Ops:
  152.7 57.6 %copy-start = (f32[4,128]{1,0:T(4,128)S(1)}, f32[4,128]{1,0:T(4,128)}, u32[]{:S(2)}) copy-start(f32[4,128]{1,0:T(4,128)} %get-tuple-element.31) | copy-start | bytes 6148

commit v6 on v5

--- a/solution.py
+++ b/solution.py
@@ -145,29 +145,28 @@
     def _():
         gs[LMAX] = picked(cotangent)
 
-    @pl.when(jnp.logical_or(first, last))
-    def _():
-        pl.semaphore_wait(barrier, 2 * (RING - 1) + 1)
-
-    @pl.when(jnp.logical_not(jnp.logical_or(first, last)))
-    def _():
-        pl.semaphore_wait(barrier, 2 * (RING - 1) + 2)
-
     mask[...] = jnp.zeros((8, BLK), F32)
     mask[:LMAX, :OWN] = (asked_ref[...] == 1).astype(F32)
     row_tiles[py] = mask[...]
-    for move in row_moves():
-        move.start()
-
-    def after_part(part):
-        if part == 1:
-            for move in row_moves():
-                move.wait()
-            all_tiles[px] = row_tiles[...]
-            for move in all_moves():
-                move.start()
+
+    def meet():
+        @pl.when(jnp.logical_or(first, last))
+        def _():
+            pl.semaphore_wait(barrier, 2 * (RING - 1) + 1)
+
+        @pl.when(jnp.logical_not(jnp.logical_or(first, last)))
+        def _():
+            pl.semaphore_wait(barrier, 2 * (RING - 1) + 2)
+
+        for move in row_moves():
+            move.start()
 
     def settle():
+        for move in row_moves():
+            move.wait()
+        all_tiles[px] = row_tiles[...]
+        for move in all_moves():
+            move.start()
         for move in all_moves():
             move.wait()
         count = jnp.zeros((1, 1), F32)
@@ -219,7 +218,8 @@
             return carry
 
         lax.fori_loop(0, NB // cols, place, 0)
-        after_part(part)
+        if part == 1:
+            meet()
         if part + 2 < PARTS:
             load(part + 2).start()
 
@@ -284,9 +284,22 @@
 
         return carry
 
+    def turn_matrix(source, target):
+        def flip(i, c):
+            rs = cols_of(i, SQ)
+            for j in range(source.shape[1] // SQ):
+                target[j * SQ:(j + 1) * SQ, rs] = source[rs, j * SQ:(j + 1) * SQ].T
+            return c
+
+        lax.fori_loop(0, source.shape[0] // SQ, flip, 0, unroll=FLIP)
+
     @pl.when(jnp.logical_not(first))
     def _():
         settle()
+
+    @pl.when(last)
+    def _():
+        turn_matrix(down_1, spare)
 
     lax.fori_loop(0, MICRO, forward, 0)
 
@@ -321,14 +334,12 @@
     def _():
         keep_left()
 
-    for source, target in ((down_1, spare), (up_1, down_1), (down_0, up_1), (up_0, down_0)):
-        def flip(i, c, source=source, target=target):
-            rs = cols_of(i, SQ)
-            for j in range(source.shape[1] // SQ):
-                target[j * SQ:(j + 1) * SQ, rs] = source[rs, j * SQ:(j + 1) * SQ].T
-            return c
-
-        lax.fori_loop(0, source.shape[0] // SQ, flip, 0, unroll=FLIP)
+    @pl.when(jnp.logical_not(last))
+    def _():
+        turn_matrix(down_1, spare)
+
+    for source, target in ((up_1, down_1), (down_0, up_1), (up_0, down_0)):
+        turn_matrix(source, target)
 
     def save_right(l):
         return pltpu.make_async_copy(right.at[l], right_hbm.at[l], right_sem.at[l])
@@ -387,7 +398,7 @@
     def _():
         pass_down().start()
 
-    most_out[...] = most[...]
+    most_out[...] = most[:1, :1]
 
     for l in range(LMAX):
         save_right(l).start()
@@ -429,7 +440,7 @@
             jax.ShapeDtypeStruct((LMAX, PANELS, KMAX, BLK), BF16),
             jax.ShapeDtypeStruct((LMAX, 8, WIDE), jnp.int32),
             jax.ShapeDtypeStruct((2 * LMAX, BLK), F32),
-            jax.ShapeDtypeStruct((8, BLK), F32),
+            jax.ShapeDtypeStruct((1, 1), F32),
         ),
         in_specs=[smem] + [vmem] * 9 + [hbm] * 2,
         out_specs=(hbm, hbm, vmem, vmem, vmem),
@@ -555,13 +566,20 @@
             send(h, 7, c, mid[h].at[c, at(second, 3)], jb[h].at[c], second, 3),
         )
 
-    def far_units(c, carry):
+    def far_blocks(c):
         for h in range(2):
             for g in range(RING):
                 opp[h][c, g] = block(h, at(h, 2), c, g).astype(BF16)
+
+    def far_sends(c):
+        for h in range(2):
             moves = copies(h, c)
             moves[0].start()
             moves[1].start()
+
+    def far_units(c, carry):
+        far_blocks(c)
+        far_sends(c)
         return carry
 
     def near_units(c, carry):
@@ -616,7 +634,7 @@
             moves[6].wait_recv()
             moves[7].wait_recv()
             v = mid[h][c, place[1 - h]].astype(F32) + ja[h][c].astype(F32) + jb[h][c].astype(F32)
-            squares[h, pl.ds(c, 1), :] = jnp.sum(v * v, axis=0, keepdims=True)
+            squares[pl.ds(h * (TILE // 2) + c, 1), :] = jnp.sum(v * v, axis=0, keepdims=True)
         return carry
 
     def drain(c, carry):
@@ -629,8 +647,8 @@
     for step in (far_units, near_units, own_units, second_axis, totals):
         lax.fori_loop(0, PER, step, 0)
     rows_total = float(RING * RING * KMAX)
-    mean = jnp.sum(squares[...].reshape(TILE, BLK), axis=1, keepdims=True) * (1.0 / (BLK * BLK))
-    mine[...] = jnp.broadcast_to(jnp.sqrt(mean / rows_total + EPS_SCORE), (TILE, BLK))
+    mean = jnp.sum(squares[...].T, axis=0, keepdims=True) * (1.0 / (BLK * BLK))
+    mine[...] = jnp.broadcast_to(jnp.sqrt(mean / rows_total + EPS_SCORE), (8, BLK))
 
     all_tiles[replica] = mine[...]
 
@@ -644,7 +662,7 @@
         tile(step).start()
     for step in range(1, everyone):
         tile(step).wait()
-    out_ref[...] = all_tiles[...]
+    out_ref[...] = all_tiles[:, 0, :]
     lax.fori_loop(0, PER, drain, 0)
 
 
@@ -658,7 +676,7 @@
 
     return pl.pallas_call(
         functools.partial(sums_kernel, PER),
-        out_shape=jax.ShapeDtypeStruct((RING * RING, TILE, BLK), F32),
+        out_shape=jax.ShapeDtypeStruct((RING * RING, BLK), F32),
         in_specs=[smem] + [hbm] * 2,
         out_specs=pl.BlockSpec(memory_space=pltpu.VMEM),
         scratch_shapes=[
@@ -667,9 +685,9 @@
             *blocks(RING, BLK), *blocks(RING, BLK), *blocks(RING, BLK), *blocks(RING, BLK),
             *blocks(2, BLK), *blocks(2, BLK), *blocks(RING, BLK), *blocks(RING, BLK),
             *blocks(HALF), *blocks(HALF), *blocks(BLK), *blocks(BLK),
-            pltpu.VMEM((2, TILE // 2, BLK), F32),
-            pltpu.VMEM((TILE, BLK), F32),
-            pltpu.VMEM((RING * RING, TILE, BLK), F32),
+            pltpu.VMEM((BLK, BLK), F32),
+            pltpu.VMEM((8, BLK), F32),
+            pltpu.VMEM((RING * RING, 8, BLK), F32),
             pltpu.SemaphoreType.DMA((2, 2)),
             pltpu.SemaphoreType.DMA((2, 8, PER)),
             pltpu.SemaphoreType.DMA((2, 8, PER)),
@@ -686,7 +704,7 @@
     per = size // (RING * RING)
     tiles = sums(size, number, slots, left, right)
     half = TILE // 2
-    tiles = tiles[:, :, 0].reshape(RING, RING, TILE)
+    tiles = tiles[:, :TILE].reshape(RING, RING, TILE)
     late = tiles[:, :, :per].transpose(0, 2, 1).reshape(size)
     early = tiles[:, :, half:half + per].transpose(1, 2, 0).reshape(size)
     return jnp.pad(jnp.stack([early, late]), ((0, 0), (0, MOST - size)))

time: 212 us -> 206 us (0.972)
  Pallas kernels: 203 us -> 199 us
    pallas_call x1, Pallas kernels: 147 us -> 142 us  [chain(): pl.pallas_call(chain_kernel, out_shape=(jax.ShapeDtypeStruct((LMAX, PANEL...]
where the time goes in v6:
time: 206 us
  Pallas kernels  199 us (97%)
  other arithmetic  2.34 us (1%)
  local copies, waits for them, and re-layouts  2.21 us (1%)
    pallas_call x1, Pallas kernels, chain(): pl.pallas_call(chain_kernel, out_shape=(jax.ShapeDtypeStruct((LMAX, PANEL...  142 us
    pallas_call x1, Pallas kernels, sums(): pl.pallas_call(functools.partial(sums_kernel, PER), out_shape=jax.ShapeDt...  57.4 us

profile of v6, /device:TPU:0, one launch (start us, length us, event | category | flops | bytes accessed | tf_op | source)
XLA Modules:
  0.0 206.2 jit_solution(18168966448364263474)
XLA Ops:
  0.0 0.7 pad_add_fusion
  0.7 0.1 fusion
  0.8 0.1 select_reduce_fusion
  1.0 0.7 select_n.22.inv_ref
  1.7 0.1 convert_element_type.21
  1.8 0.6 pad_convert_fusion.dead
  3.7 142.1 %shard_map.118 = (bf16[2,30,128,192]{3,2,1,0:T(8,128)(2,1)}, bf16[2,30,192,128]{3,2,1,0:T(8,128)(2,1)S(1)}, s32[2,8,256]{2,1,0:T(8,128)S(1)}, f32[4,128]{1,0:T(4,128)}, f32[1,1]{1,0:T(1,128)}) custom-call(s32[800]{0:T(1024)} %select_n.22.inv_ref, s32[1,1]{1,0:T(1,128)} %bitcast.17.count_ref, s32[1,256]{1,0:T(1,128)} %order.1, s32[1,1]{1,0:T(1,128)} %bitcast.16.kept, ...), custom_call_target="tpu_custom_call" | custom-call | flops 35000000512 | bytes 30000000 | tf_op jit(solution)/shard_map/pallas_call | solution.py:436
  146.3 0.0 copy-start
  146.3 58.9 %conditional.1 = (f32[2,208]{1,0:T(2,128)S(1)}) conditional(s32[]{:T(128)} %bitcast.13, (s32[2,8,256]{2,1,0:T(8,128)S(1)}, bf16[2,30,128,192]{3,2,1,0:T(8,128)(2,1)}, bf16[2,30,192,128]{3,2,1,0:T(8,128)(2,1)S(1)}) %tuple.11, (s32[2,8,256]{2,1,0:T(8,128)S(1)}, bf16[2,30,128,192]{3,2,1,0:T(8,128)(2,1)}, bf16[2,30,192,128]{3,2,1,0:T(8,128)(2,1)S(1)}) %tuple.11), branch_computations={%region_2.3_spmd, %region_3.4_spmd} | conditional | flops 3000001536 | bytes 8013320 | solution.py:736
  146.6 57.4 %branch_1_fun.1 = f32[16,128]{1,0:T(8,128)} custom-call(s32[2,8,256]{2,1,0:T(8,128)S(1)} %get-tuple-element.23.slots, bf16[2,30,128,192]{3,2,1,0:T(8,128)(2,1)} %get-tuple-element.24.left_hbm, bf16[2,30,192,128]{3,2,1,0:T(8,128)(2,1)S(1)} %get-tuple-element.25.right_hbm), custom_call_target="tpu_custom_call" | custom-call | flops 3000000000 | bytes 8000000 | tf_op jit(solution)/shard_map/cond/branch_1_fun/pallas_call | solution.py:677
  203.9 0.8 fusion.3
  204.8 0.1 copy.31
  204.9 0.1 reshape.42
  205.0 0.1 copy.32
  205.1 0.1 reshape.43
  205.2 0.0 copy-done
  205.2 0.1 copy.27
  205.3 0.2 fusion.1
  205.5 0.1 copy.28
  205.6 0.6 compare_select_fusion.1
  (6 shorter events, 0.0 us)
Async XLA Ops:
  146.3 58.9 %copy-start = (f32[4,128]{1,0:T(4,128)S(1)}, f32[4,128]{1,0:T(4,128)}, u32[]{:S(2)}) copy-start(f32[4,128]{1,0:T(4,128)} %get-tuple-element.31) | copy-start | bytes 6148

commit v7 on v6

--- a/solution.py
+++ b/solution.py
@@ -379,6 +379,10 @@
             for b in range(DOWN_COLS):
                 right[l, UP_COLS + b, r, :] = had[:, b * BLK:(b + 1) * BLK]
             gs[l, r, :] = jnp.where(flag(l), (had.astype(F32) + step).astype(BF16), had)
+            if l > 0:
+                @pl.when(mb == MICRO - 1)
+                def _(l=l):
+                    save_right(l).start()
 
         @pl.when(jnp.logical_not(first))
         def _():
@@ -400,8 +404,7 @@
 
     most_out[...] = most[:1, :1]
 
-    for l in range(LMAX):
-        save_right(l).start()
+    save_right(0).start()
 
     @pl.when(last)
     def _():

time: 206 us -> 210 us (1.019)
  Pallas kernels: 199 us -> 203 us
    pallas_call x1, Pallas kernels: 142 us -> 145 us  [chain(): pl.pallas_call(chain_kernel, out_shape=(jax.ShapeDtypeStruct((LMAX, PANEL...]
where the time goes in v7:
time: 210 us; the launch traced here: 209 us
  Pallas kernels  203 us (97%)
  other arithmetic  2.34 us (1%)
  local copies, waits for them, and re-layouts  2.21 us (1%)
    pallas_call x1, Pallas kernels, chain(): pl.pallas_call(chain_kernel, out_shape=(jax.ShapeDtypeStruct((LMAX, PANEL...  145 us
    pallas_call x1, Pallas kernels, sums(): pl.pallas_call(functools.partial(sums_kernel, PER), out_shape=jax.ShapeDt...  57.3 us

profile of v7, /device:TPU:0, one launch (start us, length us, event | category | flops | bytes accessed | tf_op | source)
XLA Modules:
  0.0 209.5 jit_solution(3821608284866354649)
XLA Ops:
  0.0 0.7 pad_add_fusion
  0.7 0.1 fusion
  0.8 0.1 select_reduce_fusion
  1.0 0.7 select_n.22.inv_ref
  1.7 0.1 convert_element_type.21
  1.8 0.6 pad_convert_fusion.dead
  3.7 145.5 %shard_map.118 = (bf16[2,30,128,192]{3,2,1,0:T(8,128)(2,1)}, bf16[2,30,192,128]{3,2,1,0:T(8,128)(2,1)S(1)}, s32[2,8,256]{2,1,0:T(8,128)S(1)}, f32[4,128]{1,0:T(4,128)}, f32[1,1]{1,0:T(1,128)}) custom-call(s32[800]{0:T(1024)} %select_n.22.inv_ref, s32[1,1]{1,0:T(1,128)} %bitcast.17.count_ref, s32[1,256]{1,0:T(1,128)} %order.1, s32[1,1]{1,0:T(1,128)} %bitcast.16.kept, ...), custom_call_target="tpu_custom_call" | custom-call | flops 35000000512 | bytes 30000000 | tf_op jit(solution)/shard_map/pallas_call | solution.py:439
  149.7 0.0 copy-start
  149.7 58.8 %conditional.1 = (f32[2,208]{1,0:T(2,128)S(1)}) conditional(s32[]{:T(128)} %bitcast.13, (s32[2,8,256]{2,1,0:T(8,128)S(1)}, bf16[2,30,128,192]{3,2,1,0:T(8,128)(2,1)}, bf16[2,30,192,128]{3,2,1,0:T(8,128)(2,1)S(1)}) %tuple.11, (s32[2,8,256]{2,1,0:T(8,128)S(1)}, bf16[2,30,128,192]{3,2,1,0:T(8,128)(2,1)}, bf16[2,30,192,128]{3,2,1,0:T(8,128)(2,1)S(1)}) %tuple.11), branch_computations={%region_2.3_spmd, %region_3.4_spmd} | conditional | flops 3000001536 | bytes 8013320 | solution.py:739
  150.0 57.3 %branch_1_fun.1 = f32[16,128]{1,0:T(8,128)} custom-call(s32[2,8,256]{2,1,0:T(8,128)S(1)} %get-tuple-element.23.slots, bf16[2,30,128,192]{3,2,1,0:T(8,128)(2,1)} %get-tuple-element.24.left_hbm, bf16[2,30,192,128]{3,2,1,0:T(8,128)(2,1)S(1)} %get-tuple-element.25.right_hbm), custom_call_target="tpu_custom_call" | custom-call | flops 3000000000 | bytes 8000000 | tf_op jit(solution)/shard_map/cond/branch_1_fun/pallas_call | solution.py:680
  207.2 0.8 fusion.3
  208.1 0.1 copy.31
  208.2 0.1 reshape.42
  208.3 0.1 copy.32
  208.4 0.1 reshape.43
  208.5 0.0 copy-done
  208.5 0.1 copy.27
  208.6 0.2 fusion.1
  208.8 0.1 copy.28
  208.9 0.6 compare_select_fusion.1
  (6 shorter events, 0.0 us)
Async XLA Ops:
  149.7 58.8 %copy-start = (f32[4,128]{1,0:T(4,128)S(1)}, f32[4,128]{1,0:T(4,128)}, u32[]{:S(2)}) copy-start(f32[4,128]{1,0:T(4,128)} %get-tuple-element.31) | copy-start | bytes 6148
